TPU v7x, 128 devices: a whole 4x4x4 slice. The times are simulated.
128 devices in a mesh: morton: 32 (over y, x, core), level: 4 (over z).
Axes of the slice: x: 4, y: 4, z: 4, core: 2. Of those that a mesh axis runs over, the one named last changes fastest.
Arguments:
- coef: float32 [131072, 512], P(('morton', 'level')), may hold values from -6 to 6
- mask: int32 [131072], P(('morton', 'level')), may hold values from 0 to 1, as said below
- neighbours: int32 [131072, 2], P(('morton', 'level')), may hold values from -1 to 131071, as said below
- two_scale: float32 [16, 16], replicated, may hold values from -1.5 to 1.5
- deriv_blocks: float32 [3, 8, 8], replicated, may hold values from -1.25 to 1.25
Outputs:
- wavelet_coef: float32 [131072, 512], P(('morton', 'level'))
- derivative: float32 [131072, 512], P(('morton', 'level'))
Inputs may be any that keep to these rules, and one draw needn't show every extreme that they name: `mask`: aligned groups of 8 boxes (families) share one value; in each aligned tile of 128 boxes the live families come first, and half of them or more are live. `neighbours`: device ranks follow box indices in blocks of 1024. An entry on its box's own device is the box just before (left) or after (right) it, or -1 at the device's first or last box. Of the 2048 entries of one device's boxes, at most 8 lie on any one other device, exactly 8 on some other device, and they lie on exactly 127 other devices.
All inputs are finite; a program needn't handle non-finite values.
Results may differ from a plain program's by a relative error of at most 0.0003.
Values sent between devices are 32-bit elements; how exact they have to be, the bound alone decides.
No kernel may reach another device: no remote copies, remote signals or barrier semaphores. Data moves between devices by JAX's collectives and lax.ppermute only.
A program may use at most 192 MiB of HBM per device.

v0:
```python
import jax
import jax.numpy as jnp
from jax import lax
from jax.experimental import pallas as pl
from jax.experimental.pallas import tpu as pltpu
from jax.sharding import PartitionSpec as P

ORDER = 8
COEFS = 512
SQ = ORDER * ORDER
LANES = 128
CHUNKS = COEFS // LANES
TILE = 128
CAP = 8
AXES = ("morton", "level")
F32 = jnp.float32
BF16 = jnp.bfloat16
I32 = jnp.int32


def iota(shape, dim):
    return lax.broadcasted_iota(I32, shape, dim)


def dot(a, b, dims=((1,), (0,))):
    return lax.dot_general(a, b, (dims, ((), ())), preferred_element_type=F32)


def split(x):
    high = x.astype(BF16)
    return high, (x - high.astype(F32)).astype(BF16)


def route_kernel(rank_ref, near_ref, mask_ref, request_ref, ghost_ref, local_ref):
    boxes = near_ref.shape[1]
    peers = request_ref.shape[0]
    part = 256
    rank = rank_ref[0]
    tri_row, tri_col = iota((part, 2 * part), 0), iota((part, 2 * part), 1)
    tri = ((tri_row < tri_col) | (tri_col >= part)).astype(F32).astype(BF16)
    peer_ids = iota((peers, part), 0)
    slot_ids = iota((CAP, part), 0)
    carry = jnp.zeros((peers, part), F32)
    high_sum = jnp.zeros((peers, CAP), F32)
    low_sum = jnp.zeros((peers, CAP), F32)
    for side in range(2):
        for start in range(0, boxes, part):
            span = pl.ds(start, part)
            entry = near_ref[pl.ds(side, 1), span]
            live = mask_ref[:, span] > 0
            owner = lax.shift_right_arithmetic(entry, 10)
            row = lax.bitwise_and(entry, boxes - 1) + side * boxes
            mine = owner == rank
            remote = (owner >= 0) & (~mine) & live
            local_ref[pl.ds(side, 1), span] = (mine & live).astype(F32)
            target = jnp.where(remote, owner, -1)
            hot_mask = peer_ids == target
            hot_f = hot_mask.astype(F32)
            hot = hot_f.astype(BF16)
            counted = dot(hot, tri)
            before = counted[:, :part] + carry
            carry = carry + counted[:, part:]
            slot = jnp.sum(hot_f * before, axis=0, keepdims=True).astype(I32)
            ghost_ref[pl.ds(side, 1), span] = jnp.where(
                remote, owner * CAP + slot, rank * CAP
            )
            picked = slot_ids == slot
            high = lax.shift_right_logical(row, 6).astype(F32)
            low = lax.bitwise_and(row, 63).astype(F32)
            high_sum += dot(hot, jnp.where(picked, high, 0.0).astype(BF16), ((1,), (1,)))
            low_sum += dot(hot, jnp.where(picked, low, 0.0).astype(BF16), ((1,), (1,)))
    request = (high_sum * 64.0 + low_sum).astype(I32)
    request_ref[...] = request.reshape(peers, 1, CAP)


def route(rank, near, mask_row, peers):
    boxes = near.shape[1]
    vmem = pl.BlockSpec(memory_space=pltpu.VMEM)
    return pl.pallas_call(
        route_kernel,
        in_specs=[pl.BlockSpec(memory_space=pltpu.SMEM), vmem, vmem],
        out_specs=[vmem, vmem, vmem],
        out_shape=[
            jax.ShapeDtypeStruct((peers, 1, CAP), I32),
            jax.ShapeDtypeStruct((2, boxes), I32),
            jax.ShapeDtypeStruct((2, boxes), F32),
        ],
        name="route",
    )(rank, near, mask_row)


def fill_weights(blocks_ref, weight_ref, sides):
    first_half = iota((8, LANES), 1) < SQ
    for n, side in enumerate(sides):
        for i in range(CHUNKS):
            for j in range(CHUNKS):
                def at(di, dj):
                    return blocks_ref[side, (2 * i + di) * ORDER + 2 * j + dj]

                k = ((n * CHUNKS + i) * CHUNKS + j) * 2
                weight_ref[k] = jnp.where(first_half, at(0, 0), at(1, 1))
                weight_ref[k + 1] = jnp.where(first_half, at(0, 1), at(1, 0))


def live_count(mask_ref, tile):
    total = jnp.int32(0)
    for family in range(TILE // 8):
        total += mask_ref[tile * TILE + family * 8]
    return total * 8


def apply_blocks(coef_ref, weight_ref, live, count, put, rows=32):
    def step(r, carry):
        start = pl.multiple_of(r * rows, rows)
        alive = (iota((rows, LANES), 0) + start) < live
        straight, swapped = [], []
        for j in range(CHUNKS):
            x = coef_ref[pl.ds(start, rows), pl.ds(j * LANES, LANES)]
            x = jnp.where(alive, x, 0.0)
            straight.append(x.reshape(rows // 8, 8, LANES))
            swapped.append(pltpu.roll(x, SQ, 1).reshape(rows // 8, 8, LANES))
        for n in range(count):
            for i in range(CHUNKS):
                total = None
                for j in range(CHUNKS):
                    k = ((n * CHUNKS + i) * CHUNKS + j) * 2
                    term = (
                        weight_ref[k][None] * straight[j]
                        + weight_ref[k + 1][None] * swapped[j]
                    )
                    total = term if total is None else total + term
                put(n, i, start, total.reshape(rows, LANES))
        return carry

    lax.fori_loop(0, TILE // rows, step, 0)


def table_kernel(mask_ref, blocks_ref, coef_ref, table_ref, weight_ref):
    tile = pl.program_id(0)

    @pl.when(tile == 0)
    def _():
        fill_weights(blocks_ref, weight_ref, (0, 2))

    def put(n, i, start, value):
        rows = value.shape[0]
        table_ref[n, pl.ds(start * CHUNKS + i, rows, stride=CHUNKS), :] = value

    apply_blocks(coef_ref, weight_ref, live_count(mask_ref, tile), 2, put)


def make_table(mask, blocks, coef):
    boxes = coef.shape[0]
    smem = pl.BlockSpec(memory_space=pltpu.SMEM)
    return pl.pallas_call(
        table_kernel,
        grid=(boxes // TILE,),
        in_specs=[smem, smem, pl.BlockSpec((TILE, COEFS), lambda t: (t, 0))],
        out_specs=pl.BlockSpec((2, TILE * CHUNKS, LANES), lambda t: (0, t, 0)),
        out_shape=jax.ShapeDtypeStruct((2, boxes * CHUNKS, LANES), F32),
        scratch_shapes=[pltpu.VMEM((2 * CHUNKS * CHUNKS * 2, 8, LANES), F32)],
        cost_estimate=pl.CostEstimate(
            flops=boxes * COEFS * 32, bytes_accessed=boxes * COEFS * 12, transcendentals=0
        ),
        name="table",
    )(mask, blocks, coef)


def serve_kernel(rank_ref, request_ref, table_ref, reply_ref):
    peers = reply_ref.shape[0] // (CAP * CHUNKS)
    first = pl.program_id(0) * peers

    def step(p, carry):
        for s in range(CAP):
            row = request_ref[first + p, 0, s]
            reply_ref[pl.ds((p * CAP + s) * CHUNKS, CHUNKS), :] = table_ref[
                pl.ds(row * CHUNKS, CHUNKS), :
            ]
        return carry

    lax.fori_loop(0, peers, step, 0, unroll=4)
    own = rank_ref[0] - first

    @pl.when((own >= 0) & (own < peers))
    def _():
        span = CAP * CHUNKS
        reply_ref[pl.ds(pl.multiple_of(own * span, span), span), :] = jnp.zeros(
            (span, LANES), F32
        )


def serve(rank, request, table):
    peers = request.shape[0]
    steps = 4
    smem = pl.BlockSpec(memory_space=pltpu.SMEM)
    return pl.pallas_call(
        serve_kernel,
        grid=(steps,),
        in_specs=[smem, smem, pl.BlockSpec(memory_space=pltpu.VMEM)],
        out_specs=pl.BlockSpec((peers * CAP * CHUNKS // steps, LANES), lambda t: (t, 0)),
        out_shape=jax.ShapeDtypeStruct((peers * CAP * CHUNKS, LANES), F32),
        name="serve",
    )(rank, request, table)


def expand(scale, rows, cols, row_of, col_of):
    pick_row = (iota((rows, 16), 1) == row_of(iota((rows, 16), 0))).astype(F32)
    pick_col = (iota((16, cols), 0) == col_of(iota((16, cols), 1))).astype(F32)
    highest = lax.Precision.HIGHEST
    wide = jnp.dot(pick_row, scale, precision=highest, preferred_element_type=F32)
    return jnp.dot(wide, pick_col, precision=highest, preferred_element_type=F32)


def base_kernel(
    mask_ref, blocks_ref, local_ref, coef_ref, table_ref, scale_ref,
    base_ref, yz_high_ref, yz_low_ref, x_high_ref, x_low_ref, weight_ref,
):
    tile = pl.program_id(0)
    tiles = pl.num_programs(0)
    span = 2 * SQ * 2

    @pl.when(tile == 0)
    def _():
        fill_weights(blocks_ref, weight_ref, (1,))
        scale = scale_ref[...]
        scale_t = scale.T
        def bits(v, shift, mask):
            return lax.bitwise_and(lax.shift_right_logical(v, shift), mask)

        def y_of(v):
            return bits(v, 7, 1) * 8 + bits(v, 3, 7)

        def z_of(v):
            return bits(v, 6, 1) * 8 + bits(v, 0, 7)

        yz = expand(scale_t, span, span, y_of, y_of) * expand(scale_t, span, span, z_of, z_of)
        yz_high_ref[...], yz_low_ref[...] = split(yz)

        def x_of(v):
            return lax.shift_right_logical(v, 4)

        wide = expand(scale, span, span, x_of, x_of)
        same = bits(iota((span, span), 0), 0, 15) == bits(iota((span, span), 1), 0, 15)
        x_high_ref[...], x_low_ref[...] = split(jnp.where(same, wide, 0.0))

    def put(n, i, start, value):
        rows = value.shape[0]
        base_ref[pl.ds(start * CHUNKS + i, rows, stride=CHUNKS), :] = value

    apply_blocks(coef_ref, weight_ref, live_count(mask_ref, tile), 1, put)
    boxes = tiles * TILE

    def add(b, carry):
        box = tile * TILE + b
        spot = pl.ds(b * CHUNKS, CHUNKS)
        left = table_ref[0, pl.ds(jnp.maximum(box - 1, 0) * CHUNKS, CHUNKS), :]
        right = table_ref[1, pl.ds(jnp.minimum(box + 1, boxes - 1) * CHUNKS, CHUNKS), :]
        base_ref[spot, :] += left * local_ref[0, box] + right * local_ref[1, box]
        return carry

    lax.fori_loop(0, TILE, add, 0, unroll=8)


def make_base(mask, blocks, local, coef, table, scale):
    boxes = coef.shape[0]
    span = 4 * SQ
    smem = pl.BlockSpec(memory_space=pltpu.SMEM)
    vmem = pl.BlockSpec(memory_space=pltpu.VMEM)
    return pl.pallas_call(
        base_kernel,
        grid=(boxes // TILE,),
        in_specs=[
            smem, smem, smem,
            pl.BlockSpec((TILE, COEFS), lambda t: (t, 0)),
            vmem, vmem,
        ],
        out_specs=[pl.BlockSpec((TILE * CHUNKS, LANES), lambda t: (t, 0)), vmem, vmem, vmem, vmem],
        out_shape=[jax.ShapeDtypeStruct((boxes * CHUNKS, LANES), F32)]
        + [jax.ShapeDtypeStruct((span, span), BF16)] * 4,
        scratch_shapes=[pltpu.VMEM((CHUNKS * CHUNKS * 2, 8, LANES), F32)],
        cost_estimate=pl.CostEstimate(
            flops=boxes * COEFS * 32, bytes_accessed=boxes * COEFS * 16, transcendentals=0
        ),
        name="base",
    )(mask, blocks, local, coef, table, scale)


def product(left, right):
    left_high, left_low = left
    right_high, right_low = right
    return (
        dot(left_high, right_high) + dot(left_low, right_high) + dot(left_high, right_low)
    )


def final_kernel(
    ghost_index_ref, ghosts_ref, base_ref, yz_high_ref, yz_low_ref, x_high_ref, x_low_ref,
    wavelet_ref, derivative_ref, rows_ref, in_high_ref, in_low_ref, out_ref,
):
    tile = pl.program_id(0)
    families = TILE // 8

    def add(b, carry):
        box = tile * TILE + b
        spot = pl.ds(b * CHUNKS, CHUNKS)
        left = ghosts_ref[pl.ds(ghost_index_ref[0, box] * CHUNKS, CHUNKS), :]
        right = ghosts_ref[pl.ds(ghost_index_ref[1, box] * CHUNKS, CHUNKS), :]
        rows_ref[spot, :] = base_ref[spot, :] + (left + right)
        return carry

    lax.fori_loop(0, TILE, add, 0, unroll=8)
    for j in range(CHUNKS):
        derivative_ref[:, pl.ds(j * LANES, LANES)] = rows_ref[pl.ds(j, TILE, stride=CHUNKS), :]
    first_half = iota((families, LANES), 1) < SQ
    for cx in range(2):
        for j in range(CHUNKS):
            for cy in range(2):
                box = cx * 4 + cy * 2
                z0 = rows_ref[pl.ds(box * CHUNKS + j, families, stride=8 * CHUNKS), :]
                z1 = rows_ref[pl.ds((box + 1) * CHUNKS + j, families, stride=8 * CHUNKS), :]
                even = jnp.where(first_half, z0, pltpu.roll(z1, SQ, 1))
                odd = jnp.where(first_half, pltpu.roll(z0, SQ, 1), z1)
                for half, value in enumerate((even, odd)):
                    spot = pl.ds((cx * 8 + 2 * j + half) * families, families)
                    lanes = pl.ds(cy * LANES, LANES)
                    high, low = split(value)
                    in_high_ref[spot, lanes] = high
                    in_low_ref[spot, lanes] = low
    middle = product(
        (in_high_ref[...], in_low_ref[...]), (yz_high_ref[...], yz_low_ref[...])
    )
    result = product((x_high_ref[...], x_low_ref[...]), split(middle))
    for ox in range(2):
        for i in range(CHUNKS):
            for oy in range(2):
                top = (ox * 8 + 2 * i) * families
                lanes = slice(oy * LANES, (oy + 1) * LANES)
                even = result[top : top + families, lanes]
                odd = result[top + families : top + 2 * families, lanes]
                z0 = jnp.where(first_half, even, pltpu.roll(odd, SQ, 1))
                z1 = jnp.where(first_half, pltpu.roll(even, SQ, 1), odd)
                box = ox * 4 + oy * 2
                out_ref[i, pl.ds(box, families, stride=8), :] = z0
                out_ref[i, pl.ds(box + 1, families, stride=8), :] = z1
    for i in range(CHUNKS):
        wavelet_ref[:, pl.ds(i * LANES, LANES)] = out_ref[i]


def finish(ghost_index, ghosts, base, matrices):
    boxes = ghost_index.shape[1]
    span = 4 * SQ
    vmem = pl.BlockSpec(memory_space=pltpu.VMEM)
    block = pl.BlockSpec((TILE, COEFS), lambda t: (t, 0))
    return pl.pallas_call(
        final_kernel,
        grid=(boxes // TILE,),
        in_specs=[
            pl.BlockSpec(memory_space=pltpu.SMEM),
            vmem,
            pl.BlockSpec((TILE * CHUNKS, LANES), lambda t: (t, 0)),
            vmem, vmem, vmem, vmem,
        ],
        out_specs=[block, block],
        out_shape=[jax.ShapeDtypeStruct((boxes, COEFS), F32)] * 2,
        scratch_shapes=[
            pltpu.VMEM((TILE * CHUNKS, LANES), F32),
            pltpu.VMEM((span, span), BF16),
            pltpu.VMEM((span, span), BF16),
            pltpu.VMEM((CHUNKS, TILE, LANES), F32),
        ],
        name="finish",
    )(ghost_index, ghosts, base, *matrices)


def exchange(x):
    return lax.all_to_all(x, AXES, split_axis=0, concat_axis=0, tiled=True)


def body(coef, mask, neighbours, two_scale, deriv_blocks):
    boxes = coef.shape[0]
    rank = lax.axis_index(AXES).astype(I32).reshape(1)
    peers = lax.axis_size("morton") * lax.axis_size("level")
    blocks = deriv_blocks.reshape(3, SQ)
    request, ghost_index, local = route(rank, neighbours.T, mask.reshape(1, boxes), peers)
    asked = exchange(request)
    table = make_table(mask, blocks, coef)
    reply = serve(rank, asked, table.reshape(2 * boxes * CHUNKS, LANES))
    ghosts = exchange(reply.reshape(peers, CAP * CHUNKS, LANES))
    base, *matrices = make_base(mask, blocks, local, coef, table, two_scale)
    return tuple(finish(ghost_index, ghosts.reshape(-1, LANES), base, matrices))


def solution(mesh):
    in_specs = (P(AXES, None), P(AXES), P(AXES, None), P(), P())
    out_specs = (P(AXES, None), P(AXES, None))
    return jax.shard_map(body, mesh=mesh, in_specs=in_specs, out_specs=out_specs, check_vma=False)
```

profile of v0, /device:TPU:1, one launch (start us, length us, event | category | flops | bytes accessed | tf_op | source)
XLA Modules:
  0.0 87.0 jit_solution(6881264210090108532)
XLA Ops:
  0.6 3.1 %route.1 = (s32[128,1,8]{2,1,0:T(1,128)}, s32[2,1024]{1,0:T(2,128)}, f32[2,1024]{1,0:T(2,128)}) custom-call(s32[1]{0:T(128)} %bitcast.rank_ref, s32[2,1024]{1,0:T(2,128)} %bitcast.10, s32[1,1024]{1,0:T(1,128)} %bitcast.9), custom_call_target="tpu_custom_call" | custom-call | tf_op jit(solution)/shard_map/route/pallas_call | solution.py:79
  3.8 11.5 %all-to-all-start = ((s32[128,1,8]{2,1,0:T(1,128)}), s32[128,1,8]{2,1,0:T(1,128)S(1)}, u32[]{:S(2)}, u32[]{:S(2)}) async-start(s32[128,1,8]{2,1,0:T(1,128)} %get-tuple-element.11), calls=%async_computation | async-start | bytes 131072 | tf_op jit(solution)/shard_map/all_to_all | solution.py:376
  15.3 1.4 %reshape.24.blocks_ref = f32[3,64]{1,0:T(4,128)} reshape(f32[3,8,8]{2,1,0:T(8,128)} %param.9) | data formatting | bytes 1536 | tf_op jit(solution)/shard_map/reshape | solution.py:383
  16.6 8.1 %table.1.table_ref = f32[2,4096,128]{2,1,0:T(8,128)} custom-call(s32[1024]{0:T(1024)} %mask_ref.3, f32[3,64]{1,0:T(4,128)} %reshape.24.blocks_ref, f32[1024,512]{1,0:T(8,128)} %coef_ref.3), custom_call_target="tpu_custom_call" | custom-call | flops 16777216 | bytes 6291456 | tf_op jit(solution)/shard_map/table/pallas_call | solution.py:155
  24.7 0.1 all-to-all-done.request_ref
  24.8 0.0 copy-start.1
  24.8 0.6 copy-done.1
  25.4 4.8 %serve.1 = f32[4096,128]{1,0:T(8,128)} custom-call(s32[1]{0:T(128)} %bitcast.rank_ref, s32[128,1,8]{2,1,0:T(1,128)} %copy-done.1, f32[8192,128]{1,0:T(8,128)} %bitcast.6), custom_call_target="tpu_custom_call" | custom-call | tf_op jit(solution)/shard_map/serve/pallas_call | solution.py:196
  30.3 9.7 %all-to-all-start.1 = ((f32[128,32,128]{2,1,0:T(8,128)}), f32[128,32,128]{2,1,0:T(8,128)S(1)}, u32[]{:S(2)}, u32[]{:S(2)}) async-start(f32[128,32,128]{2,1,0:T(8,128)} %bitcast.7), calls=%async_computation.1 | async-start | bytes 4194304 | tf_op jit(solution)/shard_map/all_to_all | solution.py:376
  39.9 14.5 %base.1 = (f32[4096,128]{1,0:T(8,128)}, bf16[256,256]{1,0:T(8,128)(2,1)}, bf16[256,256]{1,0:T(8,128)(2,1)}, bf16[256,256]{1,0:T(8,128)(2,1)}, bf16[256,256]{1,0:T(8,128)(2,1)}) custom-call(s32[1024]{0:T(1024)} %mask_ref.3, f32[3,64]{1,0:T(4,128)} %reshape.24.blocks_ref, f32[2,1024]{1,0:T(2,128)} %get-tuple-element.12.local_ref, f32[1024,512]{1,0:T(8,128)} %coef_ref.3, ...), custom_call_target="tpu_custom_call" | custom-call | flops 16777216 | bytes 8388608 | tf_op jit(solution)/shard_map/base/pallas_call | solution.py:269
  54.5 16.0 %all-to-all-done.1 = f32[128,32,128]{2,1,0:T(8,128)S(1)} async-done(((f32[128,32,128]{2,1,0:T(8,128)}), f32[128,32,128]{2,1,0:T(8,128)S(1)}, u32[]{:S(2)}, u32[]{:S(2)}) %all-to-all-start.1) | async-done | bytes 2097184 | tf_op jit(solution)/shard_map/all_to_all | solution.py:376
  70.5 0.0 copy-start
  70.5 1.3 %copy-done = f32[128,32,128]{2,1,0:T(8,128)} copy-done((f32[128,32,128]{2,1,0:T(8,128)}, f32[128,32,128]{2,1,0:T(8,128)S(1)}, u32[]{:S(2)}) %copy-start) | copy-done | bytes 2097176
  71.9 15.1 %finish.1 = (f32[1024,512]{1,0:T(8,128)}, f32[1024,512]{1,0:T(8,128)}) custom-call(s32[2,1024]{1,0:T(2,128)} %get-tuple-element.10.ghost_index_ref, f32[4096,128]{1,0:T(8,128)} %bitcast.8, f32[4096,128]{1,0:T(8,128)} %get-tuple-element.13.base_ref, bf16[256,256]{1,0:T(8,128)(2,1)} %get-tuple-element.14.yz_high_ref, ...), custom_call_target="tpu_custom_call" | custom-call | tf_op jit(solution)/shard_map/finish/pallas_call | solution.py:354
Async XLA Ops:
  3.8 21.1 %all-to-all-start = ((s32[128,1,8]{2,1,0:T(1,128)}), s32[128,1,8]{2,1,0:T(1,128)S(1)}, u32[]{:S(2)}, u32[]{:S(2)}) async-start(s32[128,1,8]{2,1,0:T(1,128)} %get-tuple-element.11), calls=%async_computation | async-start | bytes 131072 | tf_op jit(solution)/shard_map/all_to_all | solution.py:376
  24.8 0.6 copy-start.1
  30.3 40.3 %all-to-all-start.1 = ((f32[128,32,128]{2,1,0:T(8,128)}), f32[128,32,128]{2,1,0:T(8,128)S(1)}, u32[]{:S(2)}, u32[]{:S(2)}) async-start(f32[128,32,128]{2,1,0:T(8,128)} %bitcast.7), calls=%async_computation.1 | async-start | bytes 4194304 | tf_op jit(solution)/shard_map/all_to_all | solution.py:376
  70.5 1.3 %copy-start = (f32[128,32,128]{2,1,0:T(8,128)}, f32[128,32,128]{2,1,0:T(8,128)S(1)}, u32[]{:S(2)}) copy-start(f32[128,32,128]{2,1,0:T(8,128)S(1)} %all-to-all-done.1) | copy-start | bytes 6291460
where the time goes:
time: 87.5 us; the launch traced here: 87 us
  Pallas kernels  45.7 us (52%)
  starting transfers between devices  21.2 us (24%)
  waiting for transfers between devices  16.1 us (18%)
  local copies, waits for them, and re-layouts  3.35 us (4%)
    all_to_all x2, starting transfers between devices, exchange(): return lax.all_to_all(x, AXES, split_axis=0, concat_axis=0, tiled=True)  21.2 us
    all_to_all x2, waiting for transfers between devices, exchange(): return lax.all_to_all(x, AXES, split_axis=0, concat_axis=0, tiled=True)  16.1 us
    pallas_call x1, Pallas kernels, finish(): pl.pallas_call(final_kernel, grid=(boxes // TILE,), in_specs=[pl.BlockSpe...  15.1 us
    pallas_call x1, Pallas kernels, make_base(): pl.pallas_call(base_kernel, grid=(boxes // TILE,), in_specs=[smem, smem,...  14.5 us
    pallas_call x1, Pallas kernels, make_table(): pl.pallas_call(table_kernel, grid=(boxes // TILE,), in_specs=[smem, smem,...  8.11 us
    pallas_call x1, Pallas kernels, serve(): pl.pallas_call(serve_kernel, grid=(steps,), in_specs=[smem, smem, pl.Bloc...  4.8 us
    pallas_call x1, Pallas kernels, route(): pl.pallas_call(route_kernel, in_specs=[pl.BlockSpec(memory_space=pltpu.SM...  3.12 us
    unnamed x4, local copies, waits for them, and re-layouts  1.98 us
  transfers between devices with their start and end apart: 2, of which 2 were waited for; matrix products, arithmetic and copies ran while one was open for 2% of the time, Pallas kernels for 26%

commit v1 on v0

v1 whole, which is shorter than its diff:
```python
import jax
import jax.numpy as jnp
from jax import lax
from jax.experimental import pallas as pl
from jax.experimental.pallas import tpu as pltpu
from jax.sharding import PartitionSpec as P

ORDER = 8
COEFS = 512
SQ = ORDER * ORDER
LANES = 128
CHUNKS = COEFS // LANES
TILE = 128
CAP = 8
EARLY = 4
AXES = ("morton", "level")
F32 = jnp.float32
BF16 = jnp.bfloat16
I32 = jnp.int32
LIMIT = pltpu.CompilerParams(vmem_limit_bytes=24 * 1024 * 1024)
ANYWHERE = pl.BlockSpec(memory_space=pl.ANY)
VMEM_SPEC = pl.BlockSpec(memory_space=pltpu.VMEM)
SMEM_SPEC = pl.BlockSpec(memory_space=pltpu.SMEM)


def in_hbm(*arrays):
    return [pltpu.with_memory_space_constraint(x, pltpu.HBM) for x in arrays]


def iota(shape, dim):
    return lax.broadcasted_iota(I32, shape, dim)


def dot(a, b, dims=((1,), (0,))):
    return lax.dot_general(a, b, (dims, ((), ())), preferred_element_type=F32)


def split(x):
    high = x.astype(BF16)
    return high, (x - high.astype(F32)).astype(BF16)


def route_kernel(rank_ref, near_ref, mask_ref, request_ref, ghost_ref, local_ref):
    boxes = near_ref.shape[1]
    peers = request_ref.shape[0]
    part = 256
    rank = rank_ref[0]
    tri_row, tri_col = iota((part, 2 * part), 0), iota((part, 2 * part), 1)
    tri = ((tri_row < tri_col) | (tri_col >= part)).astype(F32).astype(BF16)
    peer_ids = iota((peers, part), 0)
    slot_ids = iota((CAP, part), 0)
    carry = jnp.zeros((peers, part), F32)
    sums = jnp.zeros((peers, 2 * CAP), F32)
    for side in range(2):
        for start in range(0, boxes, part):
            span = pl.ds(start, part)
            entry = near_ref[pl.ds(side, 1), span]
            live = mask_ref[:, span] > 0
            owner = lax.shift_right_arithmetic(entry, 10)
            row = lax.bitwise_and(entry, boxes - 1) + side * boxes
            mine = owner == rank
            remote = (owner >= 0) & (~mine) & live
            local_ref[pl.ds(side, 1), span] = (mine & live).astype(F32)
            target = jnp.where(remote, owner, -1)
            hot_mask = peer_ids == target
            hot_f = hot_mask.astype(F32)
            hot = hot_f.astype(BF16)
            counted = dot(hot, tri)
            before = counted[:, :part] + carry
            carry = carry + counted[:, part:]
            slot = jnp.sum(hot_f * before, axis=0, keepdims=True).astype(I32)
            ghost_ref[pl.ds(side, 1), span] = jnp.where(
                remote, owner * CAP + slot, rank * CAP
            )
            picked = slot_ids == slot
            high = lax.shift_right_logical(row, 6).astype(F32)
            low = lax.bitwise_and(row, 63).astype(F32)
            pieces = jnp.concatenate(
                [jnp.where(picked, high, 0.0), jnp.where(picked, low, 0.0)], axis=0
            )
            sums += dot(hot, pieces.astype(BF16), ((1,), (1,)))
    request = (sums[:, :CAP] * 64.0 + sums[:, CAP:]).astype(I32)
    request_ref[...] = request.reshape(peers, 1, CAP)


def route(rank, near, mask_row, peers):
    boxes = near.shape[1]
    vmem = pl.BlockSpec(memory_space=pltpu.VMEM)
    return pl.pallas_call(
        route_kernel,
        in_specs=[pl.BlockSpec(memory_space=pltpu.SMEM), vmem, vmem],
        out_specs=[vmem, vmem, vmem],
        out_shape=[
            pltpu.HBM((peers, 1, CAP), I32),
            pltpu.HBM((2, boxes), I32),
            pltpu.HBM((2, boxes), F32),
        ],
        compiler_params=LIMIT,
        name="route",
    )(rank, *in_hbm(near, mask_row))


def fill_weights(blocks_ref, weight_ref, sides):
    first_half = iota((8, LANES), 1) < SQ
    for n, side in enumerate(sides):
        for i in range(CHUNKS):
            for j in range(CHUNKS):
                def at(di, dj):
                    return blocks_ref[side, 2 * i + di, 2 * j + dj]

                k = ((n * CHUNKS + i) * CHUNKS + j) * 2
                weight_ref[k] = jnp.where(first_half, at(0, 0), at(1, 1))
                weight_ref[k + 1] = jnp.where(first_half, at(0, 1), at(1, 0))


def live_count(mask_ref, tile):
    total = jnp.int32(0)
    for family in range(TILE // 8):
        total += mask_ref[tile * TILE + family * 8]
    return total * 8


def apply_blocks(coef_ref, weight_ref, live, offset, count, put, rows=32):
    def step(r, carry):
        start = pl.multiple_of(offset + r * rows, rows)
        alive = (iota((rows, LANES), 0) + r * rows) < live
        straight, swapped = [], []
        for j in range(CHUNKS):
            x = coef_ref[pl.ds(start, rows), pl.ds(j * LANES, LANES)]
            x = jnp.where(alive, x, 0.0)
            straight.append(x.reshape(rows // 8, 8, LANES))
            swapped.append(pltpu.roll(x, SQ, 1).reshape(rows // 8, 8, LANES))
        for n in range(count):
            for i in range(CHUNKS):
                total = None
                for j in range(CHUNKS):
                    k = ((n * CHUNKS + i) * CHUNKS + j) * 2
                    term = (
                        weight_ref[k][None] * straight[j]
                        + weight_ref[k + 1][None] * swapped[j]
                    )
                    total = term if total is None else total + term
                put(n, i, start, total.reshape(rows, LANES))
        return carry

    lax.fori_loop(0, TILE // rows, step, 0)


def table_kernel(
    mask_ref, blocks_ref, coef_ref, table_ref, weight_ref, coef_vmem, table_vmem, in_sems, out_sems
):
    tiles = coef_ref.shape[0] // TILE

    def load(tile):
        span = pl.ds(pl.multiple_of(tile * TILE, TILE), TILE)
        return pltpu.make_async_copy(coef_ref.at[span], coef_vmem.at[span], in_sems.at[tile])

    def store(tile):
        span = pl.ds(pl.multiple_of(tile * TILE * CHUNKS, TILE * CHUNKS), TILE * CHUNKS)
        return pltpu.make_async_copy(
            table_vmem.at[:, span], table_ref.at[:, span], out_sems.at[tile]
        )

    for tile in range(tiles):
        load(tile).start()
    fill_weights(blocks_ref, weight_ref, (0, 2))

    def put(n, i, start, value):
        rows = value.shape[0]
        table_vmem[n, pl.ds(start * CHUNKS + i, rows, stride=CHUNKS), :] = value

    def step(tile, carry):
        load(tile).wait()
        live = live_count(mask_ref, tile)
        apply_blocks(coef_vmem, weight_ref, live, tile * TILE, 2, put)
        store(tile).start()
        return carry

    lax.fori_loop(0, tiles, step, 0)
    for tile in range(tiles):
        store(tile).wait()


def make_table(mask, blocks, coef):
    boxes = coef.shape[0]
    tiles = boxes // TILE
    return pl.pallas_call(
        table_kernel,
        in_specs=[SMEM_SPEC, SMEM_SPEC, ANYWHERE],
        out_specs=ANYWHERE,
        out_shape=pltpu.HBM((2, boxes * CHUNKS, LANES), F32),
        scratch_shapes=[
            pltpu.VMEM((2 * CHUNKS * CHUNKS * 2, 8, LANES), F32),
            pltpu.VMEM((boxes, COEFS), F32),
            pltpu.VMEM((2, boxes * CHUNKS, LANES), F32),
            pltpu.SemaphoreType.DMA((tiles,)),
            pltpu.SemaphoreType.DMA((tiles,)),
        ],
        cost_estimate=pl.CostEstimate(
            flops=boxes * COEFS * 32, bytes_accessed=boxes * COEFS * 12, transcendentals=0
        ),
        compiler_params=LIMIT,
        name="table",
    )(*in_hbm(mask, blocks, coef))


def serve_kernel(rank_ref, request_ref, table_ref, reply_ref, reply_vmem, sems):
    peers = request_ref.shape[0]
    parts = sems.shape[0]
    part = peers // parts

    def store(n):
        span = pl.ds(n * part * CAP, part * CAP)
        return pltpu.make_async_copy(reply_vmem.at[span], reply_ref.at[span], sems.at[n])

    for n in range(parts):

        def step(p, carry):
            peer = n * part + p
            for s in range(CAP):
                reply_vmem[peer * CAP + s] = table_ref[request_ref[peer, 0, s]]
            return carry

        lax.fori_loop(0, part, step, 0, unroll=True)
        own = rank_ref[0]

        @pl.when((own >= n * part) & (own < (n + 1) * part))
        def _():
            reply_vmem[pl.ds(own * CAP, CAP)] = jnp.zeros((CAP, CHUNKS, LANES), F32)

        store(n).start()
    for n in range(parts):
        store(n).wait()


def serve(rank, request, table):
    rows = request.shape[0] * CAP
    parts = 4
    return pl.pallas_call(
        serve_kernel,
        in_specs=[SMEM_SPEC, SMEM_SPEC, VMEM_SPEC],
        out_specs=ANYWHERE,
        out_shape=pltpu.HBM((rows, CHUNKS, LANES), F32),
        scratch_shapes=[
            pltpu.VMEM((rows, CHUNKS, LANES), F32),
            pltpu.SemaphoreType.DMA((parts,)),
        ],
        compiler_params=LIMIT,
        name="serve",
    )(rank, request, *in_hbm(table))


def expand(scale, rows, cols, row_of, col_of):
    pick_row = (iota((rows, 16), 1) == row_of(iota((rows, 16), 0))).astype(F32)
    pick_col = (iota((16, cols), 0) == col_of(iota((16, cols), 1))).astype(F32)
    highest = lax.Precision.HIGHEST
    wide = jnp.dot(pick_row, scale, precision=highest, preferred_element_type=F32)
    return jnp.dot(wide, pick_col, precision=highest, preferred_element_type=F32)


def base_kernel(
    mask_ref, blocks_ref, local_ref, coef_ref, table_ref, scale_ref,
    base_ref, matrix_ref, weight_ref,
):
    tile = pl.program_id(0)
    tiles = pl.num_programs(0)
    span = 2 * SQ * 2

    @pl.when(tile == 0)
    def _():
        fill_weights(blocks_ref, weight_ref, (1,))
        scale = scale_ref[...]
        scale_t = scale.T
        def bits(v, shift, mask):
            return lax.bitwise_and(lax.shift_right_logical(v, shift), mask)

        def y_of(v):
            return bits(v, 7, 1) * 8 + bits(v, 3, 7)

        def z_of(v):
            return bits(v, 6, 1) * 8 + bits(v, 0, 7)

        yz = expand(scale_t, span, span, y_of, y_of) * expand(scale_t, span, span, z_of, z_of)
        matrix_ref[0], matrix_ref[1] = split(yz)

        def x_of(v):
            return lax.shift_right_logical(v, 4)

        wide = expand(scale, span, span, x_of, x_of)
        same = bits(iota((span, span), 0), 0, 15) == bits(iota((span, span), 1), 0, 15)
        matrix_ref[2], matrix_ref[3] = split(jnp.where(same, wide, 0.0))

    def put(n, i, start, value):
        rows = value.shape[0]
        base_ref[pl.ds(start * CHUNKS + i, rows, stride=CHUNKS), :] = value

    apply_blocks(coef_ref, weight_ref, live_count(mask_ref, tile), 0, 1, put)
    boxes = tiles * TILE

    def add(b, carry):
        box = tile * TILE + b
        spot = pl.ds(b * CHUNKS, CHUNKS)
        left = table_ref[0, pl.ds(jnp.maximum(box - 1, 0) * CHUNKS, CHUNKS), :]
        right = table_ref[1, pl.ds(jnp.minimum(box + 1, boxes - 1) * CHUNKS, CHUNKS), :]
        base_ref[spot, :] += left * local_ref[0, box] + right * local_ref[1, box]
        return carry

    lax.fori_loop(0, TILE, add, 0, unroll=8)


def make_base(mask, blocks, local, coef, table, scale):
    boxes = coef.shape[0]
    span = 4 * SQ
    smem = pl.BlockSpec(memory_space=pltpu.SMEM)
    vmem = pl.BlockSpec(memory_space=pltpu.VMEM)
    return pl.pallas_call(
        base_kernel,
        grid=(boxes // TILE,),
        in_specs=[
            smem, smem, smem,
            pl.BlockSpec((TILE, COEFS), lambda t: (t, 0)),
            vmem, vmem,
        ],
        out_specs=[pl.BlockSpec((TILE * CHUNKS, LANES), lambda t: (t, 0)), vmem],
        out_shape=[pltpu.HBM((boxes * CHUNKS, LANES), F32), pltpu.HBM((4, span, span), BF16)],
        scratch_shapes=[pltpu.VMEM((CHUNKS * CHUNKS * 2, 8, LANES), F32)],
        cost_estimate=pl.CostEstimate(
            flops=boxes * COEFS * 32, bytes_accessed=boxes * COEFS * 16, transcendentals=0
        ),
        compiler_params=LIMIT,
        name="base",
    )(*in_hbm(mask, blocks, local, coef, table, scale))


def product(left, right):
    left_high, left_low = left
    right_high, right_low = right
    return (
        dot(left_high, right_high) + dot(left_low, right_high) + dot(left_high, right_low)
    )


def final_kernel(
    ghost_index_ref, ghosts_ref, base_ref, matrix_ref, wavelet_ref, derivative_ref,
    index_smem, base_vmem, rows_ref, matrix_vmem, in_high_ref, in_low_ref, out_ref,
    derivative_vmem, wavelet_vmem, index_sem, base_sem, matrix_sem, derivative_sems, wavelet_sems,
):
    families = TILE // 8
    tiles = derivative_vmem.shape[0] // TILE
    first_half = iota((families, LANES), 1) < SQ

    def derivative_copy(tile):
        span = pl.ds(tile * TILE, TILE)
        return pltpu.make_async_copy(
            derivative_vmem.at[span], derivative_ref.at[span], derivative_sems.at[tile]
        )

    def wavelet_copy(tile):
        span = pl.ds(tile * TILE, TILE)
        return pltpu.make_async_copy(
            wavelet_vmem.at[span], wavelet_ref.at[span], wavelet_sems.at[tile]
        )

    def compress_tile(tile):
        first = tile * TILE
        if tile < EARLY:
            span = pl.ds(first * CHUNKS, TILE * CHUNKS)
            rows_ref[span, :] += base_vmem[span, :]
        for j in range(CHUNKS):
            derivative_vmem[pl.ds(first, TILE), pl.ds(j * LANES, LANES)] = rows_ref[
                pl.ds(first * CHUNKS + j, TILE, stride=CHUNKS), :
            ]
        derivative_copy(tile).start()
        for cx in range(2):
            for j in range(CHUNKS):
                for cy in range(2):
                    box = first + cx * 4 + cy * 2
                    z0 = rows_ref[pl.ds(box * CHUNKS + j, families, stride=8 * CHUNKS), :]
                    z1 = rows_ref[pl.ds((box + 1) * CHUNKS + j, families, stride=8 * CHUNKS), :]
                    even = jnp.where(first_half, z0, pltpu.roll(z1, SQ, 1))
                    odd = jnp.where(first_half, pltpu.roll(z0, SQ, 1), z1)
                    for half, value in enumerate((even, odd)):
                        spot = pl.ds((cx * 8 + 2 * j + half) * families, families)
                        lanes = pl.ds(cy * LANES, LANES)
                        high, low = split(value)
                        in_high_ref[spot, lanes] = high
                        in_low_ref[spot, lanes] = low
        middle = product(
            (in_high_ref[...], in_low_ref[...]), (matrix_vmem[0], matrix_vmem[1])
        )
        result = product((matrix_vmem[2], matrix_vmem[3]), split(middle))
        for ox in range(2):
            for i in range(CHUNKS):
                for oy in range(2):
                    top = (ox * 8 + 2 * i) * families
                    lanes = slice(oy * LANES, (oy + 1) * LANES)
                    even = result[top : top + families, lanes]
                    odd = result[top + families : top + 2 * families, lanes]
                    z0 = jnp.where(first_half, even, pltpu.roll(odd, SQ, 1))
                    z1 = jnp.where(first_half, pltpu.roll(even, SQ, 1), odd)
                    box = ox * 4 + oy * 2
                    out_ref[i, pl.ds(box, families, stride=8), :] = z0
                    out_ref[i, pl.ds(box + 1, families, stride=8), :] = z1
        for i in range(CHUNKS):
            wavelet_vmem[pl.ds(first, TILE), pl.ds(i * LANES, LANES)] = out_ref[i]
        wavelet_copy(tile).start()

    index_copy = pltpu.make_async_copy(ghost_index_ref, index_smem, index_sem)
    matrix_copy = pltpu.make_async_copy(matrix_ref, matrix_vmem, matrix_sem)
    base_copy = pltpu.make_async_copy(base_ref, base_vmem, base_sem)
    index_copy.start()
    base_copy.start()
    matrix_copy.start()
    index_copy.wait()
    for tile in range(tiles):
        first = tile * TILE
        for b in range(TILE):
            box = first + b
            left = ghosts_ref[index_smem[0, box]]
            right = ghosts_ref[index_smem[1, box]]
            spot = pl.ds(box * CHUNKS, CHUNKS)
            total = left + right
            if tile >= EARLY:
                total += base_vmem[spot, :]
            rows_ref[spot, :] = total
        if tile < EARLY - 1:
            continue
        if tile == EARLY - 1:
            base_copy.wait()
            matrix_copy.wait()
        for t in range(tile + 1) if tile == EARLY - 1 else (tile,):
            compress_tile(t)
    for tile in range(tiles):
        derivative_copy(tile).wait()
        wavelet_copy(tile).wait()


def finish(ghost_index, ghosts, base, matrices):
    boxes = ghost_index.shape[1]
    span = 4 * SQ
    tiles = boxes // TILE
    return pl.pallas_call(
        final_kernel,
        in_specs=[ANYWHERE, VMEM_SPEC, ANYWHERE, ANYWHERE],
        out_specs=[ANYWHERE, ANYWHERE],
        out_shape=[jax.ShapeDtypeStruct((boxes, COEFS), F32)] * 2,
        scratch_shapes=[
            pltpu.SMEM((2, boxes), I32),
            pltpu.VMEM((boxes * CHUNKS, LANES), F32),
            pltpu.VMEM((boxes * CHUNKS, LANES), F32),
            pltpu.VMEM((4, span, span), BF16),
            pltpu.VMEM((span, span), BF16),
            pltpu.VMEM((span, span), BF16),
            pltpu.VMEM((CHUNKS, TILE, LANES), F32),
            pltpu.VMEM((boxes, COEFS), F32),
            pltpu.VMEM((boxes, COEFS), F32),
            pltpu.SemaphoreType.DMA,
            pltpu.SemaphoreType.DMA,
            pltpu.SemaphoreType.DMA,
            pltpu.SemaphoreType.DMA((tiles,)),
            pltpu.SemaphoreType.DMA((tiles,)),
        ],
        name="finish",
        compiler_params=LIMIT,
    )(*in_hbm(ghost_index), pltpu.with_memory_space_constraint(ghosts, pltpu.VMEM), *in_hbm(base, matrices))


def exchange(x):
    return lax.all_to_all(x, AXES, split_axis=0, concat_axis=0, tiled=True)


def body(coef, mask, neighbours, two_scale, deriv_blocks):
    boxes = coef.shape[0]
    rank = lax.axis_index(AXES).astype(I32).reshape(1)
    peers = lax.axis_size("morton") * lax.axis_size("level")
    request, ghost_index, local = route(rank, neighbours.T, mask.reshape(1, boxes), peers)
    asked = exchange(request)
    table = make_table(mask, deriv_blocks, coef)
    reply = serve(rank, asked, table.reshape(2 * boxes, CHUNKS, LANES))
    ghosts = exchange(reply.reshape(peers, CAP * CHUNKS, LANES))
    base, matrices = make_base(mask, deriv_blocks, local, coef, table, two_scale)
    return tuple(finish(ghost_index, ghosts.reshape(-1, CHUNKS, LANES), base, matrices))


def solution(mesh):
    in_specs = (P(AXES, None), P(AXES), P(AXES, None), P(), P())
    out_specs = (P(AXES, None), P(AXES, None))
    return jax.shard_map(body, mesh=mesh, in_specs=in_specs, out_specs=out_specs, check_vma=False)
```

time: 87.5 us -> 74.1 us (0.85)
  Pallas kernels: 45.7 us -> 35.5 us
  local copies, waits for them, and re-layouts: 3.35 us -> 0 us
  waiting for transfers between devices: 16.1 us -> 18.3 us
  starting transfers between devices: 21.2 us -> 19.1 us
    pallas_call x3, Pallas kernels: 28.1 us -> 18.7 us  [the longest x1 7.49 us: finish(): pl.pallas_call(final_kernel, in_specs=[ANYWHERE, VMEM_SPEC, ANYWHERE, ANY...]
    all_to_all x2, waiting for transfers between devices: 16.1 us -> 18.3 us  [exchange(): return lax.all_to_all(x, AXES, split_axis=0, concat_axis=0, tiled=True)]
    all_to_all x2, starting transfers between devices: 21.2 us -> 19.1 us  [exchange(): return lax.all_to_all(x, AXES, split_axis=0, concat_axis=0, tiled=True)]
    unnamed x4 -> x0, local copies, waits for them, and re-layouts: 1.98 us -> none
    reshape x1 -> x0, local copies, waits for them, and re-layouts: 1.37 us -> none  [body(): blocks = deriv_blocks.reshape(3, SQ)]
  transfers between devices with their start and end apart: 2 -> 2, of which waited for: 2 -> 2; matrix products, arithmetic and copies ran while one was open for 2% -> 0% of each run, Pallas kernels for 26% -> 30%
where the time goes in v1:
time: 74.1 us; the launch traced here: 73.6 us
  Pallas kernels  35.5 us (48%)
  starting transfers between devices  19.1 us (26%)
  waiting for transfers between devices  18.3 us (25%)
    all_to_all x2, starting transfers between devices, exchange(): return lax.all_to_all(x, AXES, split_axis=0, concat_axis=0, tiled=True)  19.1 us
    all_to_all x2, waiting for transfers between devices, exchange(): return lax.all_to_all(x, AXES, split_axis=0, concat_axis=0, tiled=True)  18.3 us
    pallas_call x1, Pallas kernels, make_base(): pl.pallas_call(base_kernel, grid=(boxes // TILE,), in_specs=[smem, smem,...  14.5 us
    pallas_call x1, Pallas kernels, finish(): pl.pallas_call(final_kernel, in_specs=[ANYWHERE, VMEM_SPEC, ANYWHERE, ANY...  7.49 us
    pallas_call x1, Pallas kernels, make_table(): pl.pallas_call(table_kernel, in_specs=[SMEM_SPEC, SMEM_SPEC, ANYWHERE], o...  7.33 us
    pallas_call x1, Pallas kernels, serve(): pl.pallas_call(serve_kernel, in_specs=[SMEM_SPEC, SMEM_SPEC, VMEM_SPEC],...  3.87 us
    pallas_call x1, Pallas kernels, route(): pl.pallas_call(route_kernel, in_specs=[pl.BlockSpec(memory_space=pltpu.SM...  2.37 us
  transfers between devices with their start and end apart: 2, of which 2 were waited for; matrix products, arithmetic and copies ran while one was open for 0% of the time, Pallas kernels for 30%

profile of v1, /device:TPU:1, one launch (start us, length us, event | category | flops | bytes accessed | tf_op | source)
XLA Modules:
  0.0 73.6 jit_solution(17186354738846903096)
XLA Ops:
  0.6 2.4 %route.1 = (s32[128,1,8]{2,1,0:T(1,128)}, s32[2,1024]{1,0:T(2,128)}, f32[2,1024]{1,0:T(2,128)}) custom-call(s32[1]{0:T(128)} %bitcast.rank_ref, s32[2,1024]{1,0:T(2,128)} %bitcast.10, s32[1,1024]{1,0:T(1,128)} %bitcast.9), custom_call_target="tpu_custom_call" | custom-call | tf_op jit(solution)/shard_map/route/pallas_call | solution.py:89
  3.0 11.5 %all-to-all-start = ((s32[128,1,8]{2,1,0:T(1,128)}), s32[128,1,8]{2,1,0:T(1,128)S(1)}, u32[]{:S(2)}, u32[]{:S(2)}) async-start(s32[128,1,8]{2,1,0:T(1,128)} %get-tuple-element.8), calls=%async_computation | async-start | bytes 131072 | tf_op jit(solution)/shard_map/all_to_all | solution.py:469
  14.5 7.3 %table.1.table_ref = f32[2,4096,128]{2,1,0:T(8,128)} custom-call(s32[1024]{0:T(1024)} %mask_ref.3, f32[3,8,8]{2,1,0:T(8,128)} %blocks_ref.3, f32[1024,512]{1,0:T(8,128)} %coef_ref.3), custom_call_target="tpu_custom_call" | custom-call | flops 16777216 | bytes 6291456 | tf_op jit(solution)/shard_map/table/pallas_call | solution.py:187
  21.8 2.2 %all-to-all-done.request_ref = s32[128,1,8]{2,1,0:T(1,128)S(1)} async-done(((s32[128,1,8]{2,1,0:T(1,128)}), s32[128,1,8]{2,1,0:T(1,128)S(1)}, u32[]{:S(2)}, u32[]{:S(2)}) %all-to-all-start) | async-done | bytes 4128 | tf_op jit(solution)/shard_map/all_to_all | solution.py:469
  24.1 3.9 %serve.1 = f32[1024,4,128]{2,1,0:T(4,128)} custom-call(s32[1]{0:T(128)} %bitcast.rank_ref, s32[128,1,8]{2,1,0:T(1,128)S(1)} %all-to-all-done.request_ref, f32[2048,4,128]{2,1,0:T(4,128)} %bitcast.7), custom_call_target="tpu_custom_call" | custom-call | tf_op jit(solution)/shard_map/serve/pallas_call | solution.py:239
  28.0 7.6 %all-to-all-start.1 = ((f32[128,32,128]{2,1,0:T(8,128)}), f32[128,32,128]{2,1,0:T(8,128)S(1)}, u32[]{:S(2)}, u32[]{:S(2)}) async-start(f32[128,32,128]{2,1,0:T(8,128)} %bitcast.8), calls=%async_computation.1 | async-start | bytes 4194304 | tf_op jit(solution)/shard_map/all_to_all | solution.py:469
  35.5 14.5 %base.1 = (f32[4096,128]{1,0:T(8,128)}, bf16[4,256,256]{2,1,0:T(8,128)(2,1)}) custom-call(s32[1024]{0:T(1024)} %mask_ref.3, f32[3,8,8]{2,1,0:T(8,128)} %blocks_ref.3, f32[2,1024]{1,0:T(2,128)} %get-tuple-element.9.local_ref, f32[1024,512]{1,0:T(8,128)} %coef_ref.3, f32[2,4096,128]{2,1,0:T(8,128)} %table.1.table_ref, f32[16,16]{1,0:T(8,128)} %scale_ref.1), custom_call_target="tpu_custom_call" | custom-call | flops 16777216 | bytes 8388608 | tf_op jit(solution)/shard_map/base/pallas_call | solution.py:316
  50.0 16.1 %all-to-all-done.1 = f32[128,32,128]{2,1,0:T(8,128)S(1)} async-done(((f32[128,32,128]{2,1,0:T(8,128)}), f32[128,32,128]{2,1,0:T(8,128)S(1)}, u32[]{:S(2)}, u32[]{:S(2)}) %all-to-all-start.1) | async-done | bytes 2097184 | tf_op jit(solution)/shard_map/all_to_all | solution.py:469
  66.1 7.5 %finish.1 = (f32[1024,512]{1,0:T(8,128)}, f32[1024,512]{1,0:T(8,128)}) custom-call(s32[2,1024]{1,0:T(2,128)} %get-tuple-element.7.ghost_index_ref, f32[1024,4,128]{2,1,0:T(4,128)S(1)} %bitcast.6, f32[4096,128]{1,0:T(8,128)} %get-tuple-element.10.base_ref, bf16[4,256,256]{2,1,0:T(8,128)(2,1)} %get-tuple-element.11.matrix_ref), custom_call_target="tpu_custom_call" | custom-call | tf_op jit(solution)/shard_map/finish/pallas_call | solution.py:442
Async XLA Ops:
  3.0 21.1 %all-to-all-start = ((s32[128,1,8]{2,1,0:T(1,128)}), s32[128,1,8]{2,1,0:T(1,128)S(1)}, u32[]{:S(2)}, u32[]{:S(2)}) async-start(s32[128,1,8]{2,1,0:T(1,128)} %get-tuple-element.8), calls=%async_computation | async-start | bytes 131072 | tf_op jit(solution)/shard_map/all_to_all | solution.py:469
  28.0 38.1 %all-to-all-start.1 = ((f32[128,32,128]{2,1,0:T(8,128)}), f32[128,32,128]{2,1,0:T(8,128)S(1)}, u32[]{:S(2)}, u32[]{:S(2)}) async-start(f32[128,32,128]{2,1,0:T(8,128)} %bitcast.8), calls=%async_computation.1 | async-start | bytes 4194304 | tf_op jit(solution)/shard_map/all_to_all | solution.py:469

commit v2 on v1

--- a/solution.py
+++ b/solution.py
@@ -13,6 +13,7 @@
 TILE = 128
 CAP = 8
 EARLY = 4
+BOUNDS = (0, 8)
 AXES = ("morton", "level")
 F32 = jnp.float32
 BF16 = jnp.bfloat16
@@ -40,11 +41,11 @@
     return high, (x - high.astype(F32)).astype(BF16)
 
 
-def route_kernel(rank_ref, near_ref, mask_ref, request_ref, ghost_ref, local_ref):
+def route_kernel(near_ref, mask_ref, request_ref, ghost_ref, local_ref):
     boxes = near_ref.shape[1]
     peers = request_ref.shape[0]
     part = 256
-    rank = rank_ref[0]
+    rank = lax.axis_index(AXES)
     tri_row, tri_col = iota((part, 2 * part), 0), iota((part, 2 * part), 1)
     tri = ((tri_row < tri_col) | (tri_col >= part)).astype(F32).astype(BF16)
     peer_ids = iota((peers, part), 0)
@@ -83,12 +84,12 @@
     request_ref[...] = request.reshape(peers, 1, CAP)
 
 
-def route(rank, near, mask_row, peers):
+def route(near, mask_row, peers):
     boxes = near.shape[1]
     vmem = pl.BlockSpec(memory_space=pltpu.VMEM)
     return pl.pallas_call(
         route_kernel,
-        in_specs=[pl.BlockSpec(memory_space=pltpu.SMEM), vmem, vmem],
+        in_specs=[vmem, vmem],
         out_specs=[vmem, vmem, vmem],
         out_shape=[
             pltpu.HBM((peers, 1, CAP), I32),
@@ -97,7 +98,7 @@
         ],
         compiler_params=LIMIT,
         name="route",
-    )(rank, *in_hbm(near, mask_row))
+    )(*in_hbm(near, mask_row))
 
 
 def fill_weights(blocks_ref, weight_ref, sides):
@@ -143,11 +144,12 @@
                 put(n, i, start, total.reshape(rows, LANES))
         return carry
 
-    lax.fori_loop(0, TILE // rows, step, 0)
+    lax.fori_loop(0, TILE // rows, step, 0, unroll=True)
 
 
 def table_kernel(
-    mask_ref, blocks_ref, coef_ref, table_ref, weight_ref, coef_vmem, table_vmem, in_sems, out_sems
+    mask_ref, blocks_ref, coef_ref, table_ref,
+    mask_smem, blocks_smem, weight_ref, coef_vmem, table_vmem, small_sems, in_sems, out_sems,
 ):
     tiles = coef_ref.shape[0] // TILE
 
@@ -161,9 +163,15 @@
             table_vmem.at[:, span], table_ref.at[:, span], out_sems.at[tile]
         )
 
+    blocks_copy = pltpu.make_async_copy(blocks_ref, blocks_smem, small_sems.at[0])
+    mask_copy = pltpu.make_async_copy(mask_ref, mask_smem, small_sems.at[1])
+    blocks_copy.start()
+    mask_copy.start()
     for tile in range(tiles):
         load(tile).start()
-    fill_weights(blocks_ref, weight_ref, (0, 2))
+    blocks_copy.wait()
+    fill_weights(blocks_smem, weight_ref, (0, 2))
+    mask_copy.wait()
 
     def put(n, i, start, value):
         rows = value.shape[0]
@@ -171,7 +179,7 @@
 
     def step(tile, carry):
         load(tile).wait()
-        live = live_count(mask_ref, tile)
+        live = live_count(mask_smem, tile)
         apply_blocks(coef_vmem, weight_ref, live, tile * TILE, 2, put)
         store(tile).start()
         return carry
@@ -186,13 +194,16 @@
     tiles = boxes // TILE
     return pl.pallas_call(
         table_kernel,
-        in_specs=[SMEM_SPEC, SMEM_SPEC, ANYWHERE],
+        in_specs=[ANYWHERE, ANYWHERE, ANYWHERE],
         out_specs=ANYWHERE,
         out_shape=pltpu.HBM((2, boxes * CHUNKS, LANES), F32),
         scratch_shapes=[
+            pltpu.SMEM(mask.shape, I32),
+            pltpu.SMEM(blocks.shape, F32),
             pltpu.VMEM((2 * CHUNKS * CHUNKS * 2, 8, LANES), F32),
             pltpu.VMEM((boxes, COEFS), F32),
             pltpu.VMEM((2, boxes * CHUNKS, LANES), F32),
+            pltpu.SemaphoreType.DMA((2,)),
             pltpu.SemaphoreType.DMA((tiles,)),
             pltpu.SemaphoreType.DMA((tiles,)),
         ],
@@ -204,8 +215,17 @@
     )(*in_hbm(mask, blocks, coef))
 
 
-def serve_kernel(rank_ref, request_ref, table_ref, reply_ref, reply_vmem, sems):
+def serve_kernel(
+    request_hbm, table_hbm, reply_ref, request_ref, table_ref, reply_vmem, in_sems, sems
+):
+    request_copy = pltpu.make_async_copy(request_hbm, request_ref, in_sems.at[0])
+    table_copy = pltpu.make_async_copy(table_hbm, table_ref, in_sems.at[1])
+    request_copy.start()
+    table_copy.start()
+    request_copy.wait()
+    table_copy.wait()
     peers = request_ref.shape[0]
+    own = lax.axis_index(AXES)
     parts = sems.shape[0]
     part = peers // parts
 
@@ -222,7 +242,6 @@
             return carry
 
         lax.fori_loop(0, part, step, 0, unroll=True)
-        own = rank_ref[0]
 
         @pl.when((own >= n * part) & (own < (n + 1) * part))
         def _():
@@ -233,21 +252,24 @@
         store(n).wait()
 
 
-def serve(rank, request, table):
+def serve(request, table):
     rows = request.shape[0] * CAP
     parts = 4
     return pl.pallas_call(
         serve_kernel,
-        in_specs=[SMEM_SPEC, SMEM_SPEC, VMEM_SPEC],
+        in_specs=[ANYWHERE, ANYWHERE],
         out_specs=ANYWHERE,
         out_shape=pltpu.HBM((rows, CHUNKS, LANES), F32),
         scratch_shapes=[
+            pltpu.SMEM(request.shape, I32),
+            pltpu.VMEM(table.shape, F32),
             pltpu.VMEM((rows, CHUNKS, LANES), F32),
+            pltpu.SemaphoreType.DMA((2,)),
             pltpu.SemaphoreType.DMA((parts,)),
         ],
         compiler_params=LIMIT,
         name="serve",
-    )(rank, request, *in_hbm(table))
+    )(request, *in_hbm(table))
 
 
 def expand(scale, rows, cols, row_of, col_of):
@@ -343,7 +365,7 @@
 def final_kernel(
     ghost_index_ref, ghosts_ref, base_ref, matrix_ref, wavelet_ref, derivative_ref,
     index_smem, base_vmem, rows_ref, matrix_vmem, in_high_ref, in_low_ref, out_ref,
-    derivative_vmem, wavelet_vmem, index_sem, base_sem, matrix_sem, derivative_sems, wavelet_sems,
+    derivative_vmem, wavelet_vmem, index_sem, base_sems, matrix_sem, derivative_sems, wavelet_sems,
 ):
     families = TILE // 8
     tiles = derivative_vmem.shape[0] // TILE
@@ -405,31 +427,38 @@
             wavelet_vmem[pl.ds(first, TILE), pl.ds(i * LANES, LANES)] = out_ref[i]
         wavelet_copy(tile).start()
 
-    index_copy = pltpu.make_async_copy(ghost_index_ref, index_smem, index_sem)
-    matrix_copy = pltpu.make_async_copy(matrix_ref, matrix_vmem, matrix_sem)
-    base_copy = pltpu.make_async_copy(base_ref, base_vmem, base_sem)
-    index_copy.start()
-    base_copy.start()
-    matrix_copy.start()
-    index_copy.wait()
-    for tile in range(tiles):
-        first = tile * TILE
-        for b in range(TILE):
-            box = first + b
+    def base_copy(n):
+        span = pl.ds(BOUNDS[n] * TILE * CHUNKS, (BOUNDS[n + 1] - BOUNDS[n]) * TILE * CHUNKS)
+        return pltpu.make_async_copy(base_ref.at[span], base_vmem.at[span], base_sems.at[n])
+
+    def gather(tile, with_base):
+        for box in range(tile * TILE, (tile + 1) * TILE):
             left = ghosts_ref[index_smem[0, box]]
             right = ghosts_ref[index_smem[1, box]]
             spot = pl.ds(box * CHUNKS, CHUNKS)
             total = left + right
-            if tile >= EARLY:
+            if with_base:
                 total += base_vmem[spot, :]
             rows_ref[spot, :] = total
-        if tile < EARLY - 1:
-            continue
-        if tile == EARLY - 1:
-            base_copy.wait()
+
+    index_copy = pltpu.make_async_copy(ghost_index_ref, index_smem, index_sem)
+    matrix_copy = pltpu.make_async_copy(matrix_ref, matrix_vmem, matrix_sem)
+    index_copy.start()
+    base_copy(0).start()
+    matrix_copy.start()
+    for n in range(1, len(BOUNDS) - 1):
+        base_copy(n).start()
+    index_copy.wait()
+    for tile in range(EARLY):
+        gather(tile, False)
+    for n in range(len(BOUNDS) - 1):
+        base_copy(n).wait()
+        if n == 0:
             matrix_copy.wait()
-        for t in range(tile + 1) if tile == EARLY - 1 else (tile,):
-            compress_tile(t)
+        for tile in range(BOUNDS[n], BOUNDS[n + 1]):
+            if tile >= EARLY:
+                gather(tile, True)
+            compress_tile(tile)
     for tile in range(tiles):
         derivative_copy(tile).wait()
         wavelet_copy(tile).wait()
@@ -455,7 +484,7 @@
             pltpu.VMEM((boxes, COEFS), F32),
             pltpu.VMEM((boxes, COEFS), F32),
             pltpu.SemaphoreType.DMA,
-            pltpu.SemaphoreType.DMA,
+            pltpu.SemaphoreType.DMA((len(BOUNDS) - 1,)),
             pltpu.SemaphoreType.DMA,
             pltpu.SemaphoreType.DMA((tiles,)),
             pltpu.SemaphoreType.DMA((tiles,)),
@@ -471,12 +500,11 @@
 
 def body(coef, mask, neighbours, two_scale, deriv_blocks):
     boxes = coef.shape[0]
-    rank = lax.axis_index(AXES).astype(I32).reshape(1)
     peers = lax.axis_size("morton") * lax.axis_size("level")
-    request, ghost_index, local = route(rank, neighbours.T, mask.reshape(1, boxes), peers)
+    request, ghost_index, local = route(neighbours.T, mask.reshape(1, boxes), peers)
     asked = exchange(request)
     table = make_table(mask, deriv_blocks, coef)
-    reply = serve(rank, asked, table.reshape(2 * boxes, CHUNKS, LANES))
+    reply = serve(asked, table.reshape(2 * boxes, CHUNKS, LANES))
     ghosts = exchange(reply.reshape(peers, CAP * CHUNKS, LANES))
     base, matrices = make_base(mask, deriv_blocks, local, coef, table, two_scale)
     return tuple(finish(ghost_index, ghosts.reshape(-1, CHUNKS, LANES), base, matrices))

time: 74.1 us -> 71.6 us (0.966)
  Pallas kernels: 35.5 us -> 31.6 us
  waiting for transfers between devices: 18.3 us -> 22.2 us
  starting transfers between devices: 19.1 us -> 16.7 us
    all_to_all x2, waiting for transfers between devices: 18.3 us -> 22.2 us  [exchange(): return lax.all_to_all(x, AXES, split_axis=0, concat_axis=0, tiled=True)]
    pallas_call x3, Pallas kernels: 13.6 us -> 11.2 us  [the longest x1 4.96 us: make_table(): pl.pallas_call(table_kernel, in_specs=[ANYWHERE, ANYWHERE, ANYWHERE], out...]
    all_to_all x2, starting transfers between devices: 19.1 us -> 16.7 us  [exchange(): return lax.all_to_all(x, AXES, split_axis=0, concat_axis=0, tiled=True)]
    pallas_call x1, Pallas kernels: 14.5 us -> 12.9 us  [make_base(): pl.pallas_call(base_kernel, grid=(boxes // TILE,), in_specs=[smem, smem,...]
  transfers between devices with their start and end apart: 2 -> 2, of which waited for: 2 -> 2; matrix products, arithmetic and copies ran while one was open for 0% -> 0% of each run, Pallas kernels for 30% -> 25%
where the time goes in v2:
time: 71.6 us; the launch traced here: 71.2 us
  Pallas kernels  31.6 us (44%)
  waiting for transfers between devices  22.2 us (31%)
  starting transfers between devices  16.7 us (23%)
    all_to_all x2, waiting for transfers between devices, exchange(): return lax.all_to_all(x, AXES, split_axis=0, concat_axis=0, tiled=True)  22.2 us
    all_to_all x2, starting transfers between devices, exchange(): return lax.all_to_all(x, AXES, split_axis=0, concat_axis=0, tiled=True)  16.7 us
    pallas_call x1, Pallas kernels, make_base(): pl.pallas_call(base_kernel, grid=(boxes // TILE,), in_specs=[smem, smem,...  12.9 us
    pallas_call x1, Pallas kernels, finish(): pl.pallas_call(final_kernel, in_specs=[ANYWHERE, VMEM_SPEC, ANYWHERE, ANY...  7.49 us
    pallas_call x1, Pallas kernels, make_table(): pl.pallas_call(table_kernel, in_specs=[ANYWHERE, ANYWHERE, ANYWHERE], out...  4.96 us
    pallas_call x1, Pallas kernels, serve(): pl.pallas_call(serve_kernel, in_specs=[ANYWHERE, ANYWHERE], out_specs=ANY...  3.86 us
    pallas_call x1, Pallas kernels, route(): pl.pallas_call(route_kernel, in_specs=[vmem, vmem], out_specs=[vmem, vmem...  2.37 us
  transfers between devices with their start and end apart: 2, of which 2 were waited for; matrix products, arithmetic and copies ran while one was open for 0% of the time, Pallas kernels for 25%

profile of v2, /device:TPU:1, one launch (start us, length us, event | category | flops | bytes accessed | tf_op | source)
XLA Modules:
  0.0 71.2 jit_solution(11999901949819601415)
XLA Ops:
  0.6 2.4 %route.1 = (s32[128,1,8]{2,1,0:T(1,128)}, s32[2,1024]{1,0:T(2,128)}, f32[2,1024]{1,0:T(2,128)}) custom-call(s32[2,1024]{1,0:T(2,128)} %bitcast.9, s32[1,1024]{1,0:T(1,128)} %bitcast.8), custom_call_target="tpu_custom_call" | custom-call | tf_op jit(solution)/shard_map/route/pallas_call | solution.py:90
  3.0 11.5 %all-to-all-start = ((s32[128,1,8]{2,1,0:T(1,128)}), s32[128,1,8]{2,1,0:T(1,128)S(1)}, u32[]{:S(2)}, u32[]{:S(2)}) async-start(s32[128,1,8]{2,1,0:T(1,128)} %get-tuple-element.8), calls=%async_computation | async-start | bytes 131072 | tf_op jit(solution)/shard_map/all_to_all | solution.py:498
  14.5 5.0 %table.1.table_ref = f32[2,4096,128]{2,1,0:T(8,128)} custom-call(s32[1024]{0:T(1024)} %mask_ref.3, f32[3,8,8]{2,1,0:T(8,128)} %blocks_ref.3, f32[1024,512]{1,0:T(8,128)} %coef_ref.3), custom_call_target="tpu_custom_call" | custom-call | flops 16777216 | bytes 6291456 | tf_op jit(solution)/shard_map/table/pallas_call | solution.py:195
  19.5 4.6 %all-to-all-done.request_hbm = s32[128,1,8]{2,1,0:T(1,128)S(1)} async-done(((s32[128,1,8]{2,1,0:T(1,128)}), s32[128,1,8]{2,1,0:T(1,128)S(1)}, u32[]{:S(2)}, u32[]{:S(2)}) %all-to-all-start) | async-done | bytes 4128 | tf_op jit(solution)/shard_map/all_to_all | solution.py:498
  24.1 3.9 %serve.1 = f32[1024,4,128]{2,1,0:T(4,128)} custom-call(s32[128,1,8]{2,1,0:T(1,128)S(1)} %all-to-all-done.request_hbm, f32[2048,4,128]{2,1,0:T(4,128)} %bitcast.6), custom_call_target="tpu_custom_call" | custom-call | tf_op jit(solution)/shard_map/serve/pallas_call | solution.py:258
  27.9 5.2 %all-to-all-start.1 = ((f32[128,32,128]{2,1,0:T(8,128)}), f32[128,32,128]{2,1,0:T(8,128)S(1)}, u32[]{:S(2)}, u32[]{:S(2)}) async-start(f32[128,32,128]{2,1,0:T(8,128)} %bitcast.7), calls=%async_computation.1 | async-start | bytes 4194304 | tf_op jit(solution)/shard_map/all_to_all | solution.py:498
  33.1 12.9 %base.1 = (f32[4096,128]{1,0:T(8,128)}, bf16[4,256,256]{2,1,0:T(8,128)(2,1)}) custom-call(s32[1024]{0:T(1024)} %mask_ref.3, f32[3,8,8]{2,1,0:T(8,128)} %blocks_ref.3, f32[2,1024]{1,0:T(2,128)} %get-tuple-element.9.local_ref, f32[1024,512]{1,0:T(8,128)} %coef_ref.3, f32[2,4096,128]{2,1,0:T(8,128)} %table.1.table_ref, f32[16,16]{1,0:T(8,128)} %scale_ref.1), custom_call_target="tpu_custom_call" | custom-call | flops 16777216 | bytes 8388608 | tf_op jit(solution)/shard_map/base/pallas_call | solution.py:338
  46.1 17.6 %all-to-all-done.1 = f32[128,32,128]{2,1,0:T(8,128)S(1)} async-done(((f32[128,32,128]{2,1,0:T(8,128)}), f32[128,32,128]{2,1,0:T(8,128)S(1)}, u32[]{:S(2)}, u32[]{:S(2)}) %all-to-all-start.1) | async-done | bytes 2097184 | tf_op jit(solution)/shard_map/all_to_all | solution.py:498
  63.7 7.5 %finish.1 = (f32[1024,512]{1,0:T(8,128)}, f32[1024,512]{1,0:T(8,128)}) custom-call(s32[2,1024]{1,0:T(2,128)} %get-tuple-element.7.ghost_index_ref, f32[1024,4,128]{2,1,0:T(4,128)S(1)} %bitcast.5, f32[4096,128]{1,0:T(8,128)} %get-tuple-element.10.base_ref, bf16[4,256,256]{2,1,0:T(8,128)(2,1)} %get-tuple-element.11.matrix_ref), custom_call_target="tpu_custom_call" | custom-call | tf_op jit(solution)/shard_map/finish/pallas_call | solution.py:471
Async XLA Ops:
  3.0 21.1 %all-to-all-start = ((s32[128,1,8]{2,1,0:T(1,128)}), s32[128,1,8]{2,1,0:T(1,128)S(1)}, u32[]{:S(2)}, u32[]{:S(2)}) async-start(s32[128,1,8]{2,1,0:T(1,128)} %get-tuple-element.8), calls=%async_computation | async-start | bytes 131072 | tf_op jit(solution)/shard_map/all_to_all | solution.py:498
  27.9 35.8 %all-to-all-start.1 = ((f32[128,32,128]{2,1,0:T(8,128)}), f32[128,32,128]{2,1,0:T(8,128)S(1)}, u32[]{:S(2)}, u32[]{:S(2)}) async-start(f32[128,32,128]{2,1,0:T(8,128)} %bitcast.7), calls=%async_computation.1 | async-start | bytes 4194304 | tf_op jit(solution)/shard_map/all_to_all | solution.py:498

commit v3 on v2

--- a/solution.py
+++ b/solution.py
@@ -124,11 +124,13 @@
 def apply_blocks(coef_ref, weight_ref, live, offset, count, put, rows=32):
     def step(r, carry):
         start = pl.multiple_of(offset + r * rows, rows)
-        alive = (iota((rows, LANES), 0) + r * rows) < live
+        if live is not None:
+            alive = (iota((rows, LANES), 0) + r * rows) < live
         straight, swapped = [], []
         for j in range(CHUNKS):
             x = coef_ref[pl.ds(start, rows), pl.ds(j * LANES, LANES)]
-            x = jnp.where(alive, x, 0.0)
+            if live is not None:
+                x = jnp.where(alive, x, 0.0)
             straight.append(x.reshape(rows // 8, 8, LANES))
             swapped.append(pltpu.roll(x, SQ, 1).reshape(rows // 8, 8, LANES))
         for n in range(count):
@@ -147,21 +149,29 @@
     lax.fori_loop(0, TILE // rows, step, 0, unroll=True)
 
 
-def table_kernel(
-    mask_ref, blocks_ref, coef_ref, table_ref,
-    mask_smem, blocks_smem, weight_ref, coef_vmem, table_vmem, small_sems, in_sems, out_sems,
+def fill_table(coef_ref, weight_ref, mask_ref, table_ref):
+    boxes = coef_ref.shape[0]
+
+    def put(n, i, start, value):
+        first = n * boxes * CHUNKS + i
+        table_ref[pl.ds(start * CHUNKS + first, value.shape[0], stride=CHUNKS), :] = value
+
+    def step(tile, carry):
+        live = None if mask_ref is None else live_count(mask_ref, tile)
+        apply_blocks(coef_ref, weight_ref, live, tile * TILE, 2, put)
+        return carry
+
+    lax.fori_loop(0, boxes // TILE, step, 0, unroll=mask_ref is None)
+
+
+def prepare_kernel(
+    mask_ref, blocks_ref, coef_ref, live_ref, weight_ref, mask_smem, blocks_smem, small_sems, sems
 ):
-    tiles = coef_ref.shape[0] // TILE
+    tiles = sems.shape[0]
 
     def load(tile):
-        span = pl.ds(pl.multiple_of(tile * TILE, TILE), TILE)
-        return pltpu.make_async_copy(coef_ref.at[span], coef_vmem.at[span], in_sems.at[tile])
-
-    def store(tile):
-        span = pl.ds(pl.multiple_of(tile * TILE * CHUNKS, TILE * CHUNKS), TILE * CHUNKS)
-        return pltpu.make_async_copy(
-            table_vmem.at[:, span], table_ref.at[:, span], out_sems.at[tile]
-        )
+        span = pl.ds(tile * TILE, TILE)
+        return pltpu.make_async_copy(coef_ref.at[span], live_ref.at[span], sems.at[tile])
 
     blocks_copy = pltpu.make_async_copy(blocks_ref, blocks_smem, small_sems.at[0])
     mask_copy = pltpu.make_async_copy(mask_ref, mask_smem, small_sems.at[1])
@@ -172,76 +182,60 @@
     blocks_copy.wait()
     fill_weights(blocks_smem, weight_ref, (0, 2))
     mask_copy.wait()
-
-    def put(n, i, start, value):
-        rows = value.shape[0]
-        table_vmem[n, pl.ds(start * CHUNKS + i, rows, stride=CHUNKS), :] = value
-
-    def step(tile, carry):
+    half = TILE // 2
+    for tile in range(tiles):
         load(tile).wait()
-        live = live_count(mask_smem, tile)
-        apply_blocks(coef_vmem, weight_ref, live, tile * TILE, 2, put)
-        store(tile).start()
-        return carry
-
-    lax.fori_loop(0, tiles, step, 0)
-    for tile in range(tiles):
-        store(tile).wait()
-
-
-def make_table(mask, blocks, coef):
+        alive = (iota((half, COEFS), 0) + half) < live_count(mask_smem, tile)
+        span = pl.ds(tile * TILE + half, half)
+        live_ref[span, :] = jnp.where(alive, live_ref[span, :], 0.0)
+
+
+def prepare(mask, blocks, coef):
     boxes = coef.shape[0]
-    tiles = boxes // TILE
     return pl.pallas_call(
-        table_kernel,
-        in_specs=[ANYWHERE, ANYWHERE, ANYWHERE],
-        out_specs=ANYWHERE,
-        out_shape=pltpu.HBM((2, boxes * CHUNKS, LANES), F32),
+        prepare_kernel,
+        in_specs=[ANYWHERE] * 3,
+        out_specs=[VMEM_SPEC] * 2,
+        out_shape=[
+            pltpu.VMEM((boxes, COEFS), F32),
+            pltpu.VMEM((2 * CHUNKS * CHUNKS * 2, 8, LANES), F32),
+        ],
         scratch_shapes=[
             pltpu.SMEM(mask.shape, I32),
             pltpu.SMEM(blocks.shape, F32),
-            pltpu.VMEM((2 * CHUNKS * CHUNKS * 2, 8, LANES), F32),
-            pltpu.VMEM((boxes, COEFS), F32),
-            pltpu.VMEM((2, boxes * CHUNKS, LANES), F32),
             pltpu.SemaphoreType.DMA((2,)),
-            pltpu.SemaphoreType.DMA((tiles,)),
-            pltpu.SemaphoreType.DMA((tiles,)),
+            pltpu.SemaphoreType.DMA((boxes // TILE,)),
         ],
         cost_estimate=pl.CostEstimate(
-            flops=boxes * COEFS * 32, bytes_accessed=boxes * COEFS * 12, transcendentals=0
+            flops=boxes * COEFS * 16, bytes_accessed=boxes * COEFS * 8, transcendentals=0
         ),
         compiler_params=LIMIT,
-        name="table",
+        name="prepare",
     )(*in_hbm(mask, blocks, coef))
 
 
 def serve_kernel(
-    request_hbm, table_hbm, reply_ref, request_ref, table_ref, reply_vmem, in_sems, sems
+    request_ref, live_ref, weight_ref, reply_ref,
+    request_smem, table_vmem, reply_vmem, request_sem, out_sems,
 ):
-    request_copy = pltpu.make_async_copy(request_hbm, request_ref, in_sems.at[0])
-    table_copy = pltpu.make_async_copy(table_hbm, table_ref, in_sems.at[1])
+    request_copy = pltpu.make_async_copy(request_ref, request_smem, request_sem)
     request_copy.start()
-    table_copy.start()
+    fill_table(live_ref, weight_ref, None, table_vmem)
     request_copy.wait()
-    table_copy.wait()
-    peers = request_ref.shape[0]
+    peers = request_smem.shape[0]
+    parts = out_sems.shape[0]
+    part = peers // parts
     own = lax.axis_index(AXES)
-    parts = sems.shape[0]
-    part = peers // parts
 
     def store(n):
         span = pl.ds(n * part * CAP, part * CAP)
-        return pltpu.make_async_copy(reply_vmem.at[span], reply_ref.at[span], sems.at[n])
+        return pltpu.make_async_copy(reply_vmem.at[span], reply_ref.at[span], out_sems.at[n])
 
     for n in range(parts):
-
-        def step(p, carry):
-            peer = n * part + p
+        for peer in range(n * part, (n + 1) * part):
             for s in range(CAP):
-                reply_vmem[peer * CAP + s] = table_ref[request_ref[peer, 0, s]]
-            return carry
-
-        lax.fori_loop(0, part, step, 0, unroll=True)
+                row = pl.multiple_of(request_smem[peer, 0, s] * CHUNKS, CHUNKS)
+                reply_vmem[peer * CAP + s] = table_vmem[pl.ds(row, CHUNKS), :]
 
         @pl.when((own >= n * part) & (own < (n + 1) * part))
         def _():
@@ -252,24 +246,24 @@
         store(n).wait()
 
 
-def serve(request, table):
+def serve(request, live, weights):
+    boxes = live.shape[0]
     rows = request.shape[0] * CAP
-    parts = 4
     return pl.pallas_call(
         serve_kernel,
-        in_specs=[ANYWHERE, ANYWHERE],
+        in_specs=[ANYWHERE, VMEM_SPEC, VMEM_SPEC],
         out_specs=ANYWHERE,
         out_shape=pltpu.HBM((rows, CHUNKS, LANES), F32),
         scratch_shapes=[
             pltpu.SMEM(request.shape, I32),
-            pltpu.VMEM(table.shape, F32),
+            pltpu.VMEM((2 * boxes * CHUNKS, LANES), F32),
             pltpu.VMEM((rows, CHUNKS, LANES), F32),
-            pltpu.SemaphoreType.DMA((2,)),
-            pltpu.SemaphoreType.DMA((parts,)),
+            pltpu.SemaphoreType.DMA,
+            pltpu.SemaphoreType.DMA((4,)),
         ],
         compiler_params=LIMIT,
         name="serve",
-    )(request, *in_hbm(table))
+    )(request, *[pltpu.with_memory_space_constraint(x, pltpu.VMEM) for x in (live, weights)])
 
 
 def expand(scale, rows, cols, row_of, col_of):
@@ -281,8 +275,8 @@
 
 
 def base_kernel(
-    mask_ref, blocks_ref, local_ref, coef_ref, table_ref, scale_ref,
-    base_ref, matrix_ref, weight_ref,
+    mask_ref, blocks_ref, local_ref, coef_ref, scale_ref,
+    base_ref, matrix_ref, weight_ref, side_weight_ref, table_ref,
 ):
     tile = pl.program_id(0)
     tiles = pl.num_programs(0)
@@ -291,6 +285,8 @@
     @pl.when(tile == 0)
     def _():
         fill_weights(blocks_ref, weight_ref, (1,))
+        fill_weights(blocks_ref, side_weight_ref, (0, 2))
+        fill_table(coef_ref, side_weight_ref, mask_ref, table_ref)
         scale = scale_ref[...]
         scale_t = scale.T
         def bits(v, shift, mask):
@@ -314,23 +310,24 @@
 
     def put(n, i, start, value):
         rows = value.shape[0]
-        base_ref[pl.ds(start * CHUNKS + i, rows, stride=CHUNKS), :] = value
-
-    apply_blocks(coef_ref, weight_ref, live_count(mask_ref, tile), 0, 1, put)
+        at = (start - tile * TILE) * CHUNKS + i
+        base_ref[pl.ds(at, rows, stride=CHUNKS), :] = value
+
+    apply_blocks(coef_ref, weight_ref, live_count(mask_ref, tile), tile * TILE, 1, put)
     boxes = tiles * TILE
 
     def add(b, carry):
         box = tile * TILE + b
         spot = pl.ds(b * CHUNKS, CHUNKS)
-        left = table_ref[0, pl.ds(jnp.maximum(box - 1, 0) * CHUNKS, CHUNKS), :]
-        right = table_ref[1, pl.ds(jnp.minimum(box + 1, boxes - 1) * CHUNKS, CHUNKS), :]
+        left = table_ref[pl.ds(jnp.maximum(box - 1, 0) * CHUNKS, CHUNKS), :]
+        right = table_ref[pl.ds((boxes + jnp.minimum(box + 1, boxes - 1)) * CHUNKS, CHUNKS), :]
         base_ref[spot, :] += left * local_ref[0, box] + right * local_ref[1, box]
         return carry
 
     lax.fori_loop(0, TILE, add, 0, unroll=8)
 
 
-def make_base(mask, blocks, local, coef, table, scale):
+def make_base(mask, blocks, local, coef, scale):
     boxes = coef.shape[0]
     span = 4 * SQ
     smem = pl.BlockSpec(memory_space=pltpu.SMEM)
@@ -340,18 +337,21 @@
         grid=(boxes // TILE,),
         in_specs=[
             smem, smem, smem,
-            pl.BlockSpec((TILE, COEFS), lambda t: (t, 0)),
             vmem, vmem,
         ],
         out_specs=[pl.BlockSpec((TILE * CHUNKS, LANES), lambda t: (t, 0)), vmem],
         out_shape=[pltpu.HBM((boxes * CHUNKS, LANES), F32), pltpu.HBM((4, span, span), BF16)],
-        scratch_shapes=[pltpu.VMEM((CHUNKS * CHUNKS * 2, 8, LANES), F32)],
+        scratch_shapes=[
+            pltpu.VMEM((CHUNKS * CHUNKS * 2, 8, LANES), F32),
+            pltpu.VMEM((2 * CHUNKS * CHUNKS * 2, 8, LANES), F32),
+            pltpu.VMEM((2 * boxes * CHUNKS, LANES), F32),
+        ],
         cost_estimate=pl.CostEstimate(
             flops=boxes * COEFS * 32, bytes_accessed=boxes * COEFS * 16, transcendentals=0
         ),
         compiler_params=LIMIT,
         name="base",
-    )(*in_hbm(mask, blocks, local, coef, table, scale))
+    )(*in_hbm(mask, blocks, local, coef, scale))
 
 
 def product(left, right):
@@ -503,10 +503,9 @@
     peers = lax.axis_size("morton") * lax.axis_size("level")
     request, ghost_index, local = route(neighbours.T, mask.reshape(1, boxes), peers)
     asked = exchange(request)
-    table = make_table(mask, deriv_blocks, coef)
-    reply = serve(asked, table.reshape(2 * boxes, CHUNKS, LANES))
+    reply = serve(asked, *prepare(mask, deriv_blocks, coef))
     ghosts = exchange(reply.reshape(peers, CAP * CHUNKS, LANES))
-    base, matrices = make_base(mask, deriv_blocks, local, coef, table, two_scale)
+    base, matrices = make_base(mask, deriv_blocks, local, coef, two_scale)
     return tuple(finish(ghost_index, ghosts.reshape(-1, CHUNKS, LANES), base, matrices))
 
 

time: 71.6 us -> 70.9 us (level)
  Pallas kernels: 31.6 us -> 30.4 us
  waiting for transfers between devices: 22.2 us -> 23.4 us
  starting transfers between devices: 16.7 us -> 15.8 us
    pallas_call x2, Pallas kernels: 8.82 us -> 5.5 us  [the longest x1 3.89 us: serve(): pl.pallas_call(serve_kernel, in_specs=[ANYWHERE, VMEM_SPEC, VMEM_SPEC], o...]
    pallas_call x1, Pallas kernels: 12.9 us -> 15.1 us  [make_base(): pl.pallas_call(base_kernel, grid=(boxes // TILE,), in_specs=[smem, smem,...]
    all_to_all x2, waiting for transfers between devices: 22.2 us -> 23.4 us  [exchange(): return lax.all_to_all(x, AXES, split_axis=0, concat_axis=0, tiled=True)]
    all_to_all x2, starting transfers between devices: 16.7 us -> 15.8 us  [exchange(): return lax.all_to_all(x, AXES, split_axis=0, concat_axis=0, tiled=True)]
  transfers between devices with their start and end apart: 2 -> 2, of which waited for: 2 -> 2; matrix products, arithmetic and copies ran while one was open for 0% -> 0% of each run, Pallas kernels for 25% -> 24%
where the time goes in v3:
time: 70.9 us; the launch traced here: 70.5 us
  Pallas kernels  30.4 us (43%)
  waiting for transfers between devices  23.4 us (33%)
  starting transfers between devices  15.8 us (22%)
  between operations  0.82 us (1%)
    all_to_all x2, waiting for transfers between devices, exchange(): return lax.all_to_all(x, AXES, split_axis=0, concat_axis=0, tiled=True)  23.4 us
    all_to_all x2, starting transfers between devices, exchange(): return lax.all_to_all(x, AXES, split_axis=0, concat_axis=0, tiled=True)  15.8 us
    pallas_call x1, Pallas kernels, make_base(): pl.pallas_call(base_kernel, grid=(boxes // TILE,), in_specs=[smem, smem,...  15.1 us
    pallas_call x1, Pallas kernels, finish(): pl.pallas_call(final_kernel, in_specs=[ANYWHERE, VMEM_SPEC, ANYWHERE, ANY...  7.5 us
    pallas_call x1, Pallas kernels, serve(): pl.pallas_call(serve_kernel, in_specs=[ANYWHERE, VMEM_SPEC, VMEM_SPEC], o...  3.89 us
    pallas_call x1, Pallas kernels, route(): pl.pallas_call(route_kernel, in_specs=[vmem, vmem], out_specs=[vmem, vmem...  2.37 us
    pallas_call x1, Pallas kernels, prepare(): pl.pallas_call(prepare_kernel, in_specs=[ANYWHERE] * 3, out_specs=[VMEM_S...  1.61 us
  transfers between devices with their start and end apart: 2, of which 2 were waited for; matrix products, arithmetic and copies ran while one was open for 0% of the time, Pallas kernels for 24%

profile of v3, /device:TPU:1, one launch (start us, length us, event | category | flops | bytes accessed | tf_op | source)
XLA Modules:
  0.0 70.5 jit_solution(549360381878579734)
XLA Ops:
  0.6 2.4 %route.1 = (s32[128,1,8]{2,1,0:T(1,128)}, s32[2,1024]{1,0:T(2,128)}, f32[2,1024]{1,0:T(2,128)}) custom-call(s32[2,1024]{1,0:T(2,128)} %bitcast.7, s32[1,1024]{1,0:T(1,128)} %bitcast.6), custom_call_target="tpu_custom_call" | custom-call | tf_op jit(solution)/shard_map/route/pallas_call | solution.py:90
  3.0 11.5 %all-to-all-start = ((s32[128,1,8]{2,1,0:T(1,128)}), s32[128,1,8]{2,1,0:T(1,128)S(1)}, u32[]{:S(2)}, u32[]{:S(2)}) async-start(s32[128,1,8]{2,1,0:T(1,128)} %get-tuple-element.10), calls=%async_computation | async-start | bytes 131072 | tf_op jit(solution)/shard_map/all_to_all | solution.py:498
  14.5 1.6 %prepare.1 = (f32[1024,512]{1,0:T(8,128)S(1)}, f32[64,8,128]{2,1,0:T(8,128)S(1)}) custom-call(s32[1024]{0:T(1024)} %mask_ref.3, f32[3,8,8]{2,1,0:T(8,128)} %blocks_ref.3, f32[1024,512]{1,0:T(8,128)} %coef_ref.3), custom_call_target="tpu_custom_call" | custom-call | flops 8388608 | bytes 4194304 | tf_op jit(solution)/shard_map/prepare/pallas_call | solution.py:195
  16.1 7.9 %all-to-all-done.request_ref = s32[128,1,8]{2,1,0:T(1,128)S(1)} async-done(((s32[128,1,8]{2,1,0:T(1,128)}), s32[128,1,8]{2,1,0:T(1,128)S(1)}, u32[]{:S(2)}, u32[]{:S(2)}) %all-to-all-start) | async-done | bytes 4128 | tf_op jit(solution)/shard_map/all_to_all | solution.py:498
  24.1 3.9 %serve.1 = f32[1024,4,128]{2,1,0:T(4,128)} custom-call(s32[128,1,8]{2,1,0:T(1,128)S(1)} %all-to-all-done.request_ref, f32[1024,512]{1,0:T(8,128)S(1)} %get-tuple-element.11.live_ref, f32[64,8,128]{2,1,0:T(8,128)S(1)} %get-tuple-element.12.weight_ref), custom_call_target="tpu_custom_call" | custom-call | tf_op jit(solution)/shard_map/serve/pallas_call | solution.py:252
  28.0 4.3 %all-to-all-start.1 = ((f32[128,32,128]{2,1,0:T(8,128)}), f32[128,32,128]{2,1,0:T(8,128)S(1)}, u32[]{:S(2)}, u32[]{:S(2)}) async-start(f32[128,32,128]{2,1,0:T(8,128)} %bitcast.5), calls=%async_computation.1 | async-start | bytes 4194304 | tf_op jit(solution)/shard_map/all_to_all | solution.py:498
  32.3 15.1 %base.1 = (f32[4096,128]{1,0:T(8,128)}, bf16[4,256,256]{2,1,0:T(8,128)(2,1)}) custom-call(s32[1024]{0:T(1024)} %mask_ref.3, f32[3,8,8]{2,1,0:T(8,128)} %blocks_ref.3, f32[2,1024]{1,0:T(2,128)} %get-tuple-element.13.local_ref, f32[1024,512]{1,0:T(8,128)} %coef_ref.3, f32[16,16]{1,0:T(8,128)} %scale_ref.1), custom_call_target="tpu_custom_call" | custom-call | flops 16777216 | bytes 8388608 | tf_op jit(solution)/shard_map/base/pallas_call | solution.py:335
  47.4 15.5 %all-to-all-done.1 = f32[128,32,128]{2,1,0:T(8,128)S(1)} async-done(((f32[128,32,128]{2,1,0:T(8,128)}), f32[128,32,128]{2,1,0:T(8,128)S(1)}, u32[]{:S(2)}, u32[]{:S(2)}) %all-to-all-start.1) | async-done | bytes 2097184 | tf_op jit(solution)/shard_map/all_to_all | solution.py:498
  62.9 7.5 %finish.1 = (f32[1024,512]{1,0:T(8,128)}, f32[1024,512]{1,0:T(8,128)}) custom-call(s32[2,1024]{1,0:T(2,128)} %get-tuple-element.9.ghost_index_ref, f32[1024,4,128]{2,1,0:T(4,128)S(1)} %bitcast.4, f32[4096,128]{1,0:T(8,128)} %get-tuple-element.14.base_ref, bf16[4,256,256]{2,1,0:T(8,128)(2,1)} %get-tuple-element.15.matrix_ref), custom_call_target="tpu_custom_call" | custom-call | tf_op jit(solution)/shard_map/finish/pallas_call | solution.py:471
Async XLA Ops:
  3.0 21.1 %all-to-all-start = ((s32[128,1,8]{2,1,0:T(1,128)}), s32[128,1,8]{2,1,0:T(1,128)S(1)}, u32[]{:S(2)}, u32[]{:S(2)}) async-start(s32[128,1,8]{2,1,0:T(1,128)} %get-tuple-element.10), calls=%async_computation | async-start | bytes 131072 | tf_op jit(solution)/shard_map/all_to_all | solution.py:498
  28.0 34.9 %all-to-all-start.1 = ((f32[128,32,128]{2,1,0:T(8,128)}), f32[128,32,128]{2,1,0:T(8,128)S(1)}, u32[]{:S(2)}, u32[]{:S(2)}) async-start(f32[128,32,128]{2,1,0:T(8,128)} %bitcast.5), calls=%async_computation.1 | async-start | bytes 4194304 | tf_op jit(solution)/shard_map/all_to_all | solution.py:498

commit v4 on v3

--- a/solution.py
+++ b/solution.py
@@ -357,15 +357,16 @@
 def product(left, right):
     left_high, left_low = left
     right_high, right_low = right
-    return (
-        dot(left_high, right_high) + dot(left_low, right_high) + dot(left_high, right_low)
+    return dot(
+        jnp.concatenate([left_high, left_low, left_high], axis=1),
+        jnp.concatenate([right_high, right_high, right_low], axis=0),
     )
 
 
 def final_kernel(
     ghost_index_ref, ghosts_ref, base_ref, matrix_ref, wavelet_ref, derivative_ref,
     index_smem, base_vmem, rows_ref, matrix_vmem, in_high_ref, in_low_ref, out_ref,
-    derivative_vmem, wavelet_vmem, index_sem, base_sems, matrix_sem, derivative_sems, wavelet_sems,
+    derivative_vmem, index_sem, base_sems, matrix_sem, derivative_sems, wavelet_sems,
 ):
     families = TILE // 8
     tiles = derivative_vmem.shape[0] // TILE
@@ -377,10 +378,10 @@
             derivative_vmem.at[span], derivative_ref.at[span], derivative_sems.at[tile]
         )
 
-    def wavelet_copy(tile):
+    def wavelet_copy(tile, i):
         span = pl.ds(tile * TILE, TILE)
         return pltpu.make_async_copy(
-            wavelet_vmem.at[span], wavelet_ref.at[span], wavelet_sems.at[tile]
+            out_ref.at[i, span], wavelet_ref.at[span, pl.ds(i * LANES, LANES)], wavelet_sems.at[tile, i]
         )
 
     def compress_tile(tile):
@@ -421,11 +422,10 @@
                     z0 = jnp.where(first_half, even, pltpu.roll(odd, SQ, 1))
                     z1 = jnp.where(first_half, pltpu.roll(even, SQ, 1), odd)
                     box = ox * 4 + oy * 2
-                    out_ref[i, pl.ds(box, families, stride=8), :] = z0
-                    out_ref[i, pl.ds(box + 1, families, stride=8), :] = z1
+                    out_ref[i, pl.ds(first + box, families, stride=8), :] = z0
+                    out_ref[i, pl.ds(first + box + 1, families, stride=8), :] = z1
         for i in range(CHUNKS):
-            wavelet_vmem[pl.ds(first, TILE), pl.ds(i * LANES, LANES)] = out_ref[i]
-        wavelet_copy(tile).start()
+            wavelet_copy(tile, i).start()
 
     def base_copy(n):
         span = pl.ds(BOUNDS[n] * TILE * CHUNKS, (BOUNDS[n + 1] - BOUNDS[n]) * TILE * CHUNKS)
@@ -461,7 +461,8 @@
             compress_tile(tile)
     for tile in range(tiles):
         derivative_copy(tile).wait()
-        wavelet_copy(tile).wait()
+        for i in range(CHUNKS):
+            wavelet_copy(tile, i).wait()
 
 
 def finish(ghost_index, ghosts, base, matrices):
@@ -480,14 +481,13 @@
             pltpu.VMEM((4, span, span), BF16),
             pltpu.VMEM((span, span), BF16),
             pltpu.VMEM((span, span), BF16),
-            pltpu.VMEM((CHUNKS, TILE, LANES), F32),
-            pltpu.VMEM((boxes, COEFS), F32),
+            pltpu.VMEM((CHUNKS, boxes, LANES), F32),
             pltpu.VMEM((boxes, COEFS), F32),
             pltpu.SemaphoreType.DMA,
             pltpu.SemaphoreType.DMA((len(BOUNDS) - 1,)),
             pltpu.SemaphoreType.DMA,
             pltpu.SemaphoreType.DMA((tiles,)),
-            pltpu.SemaphoreType.DMA((tiles,)),
+            pltpu.SemaphoreType.DMA((tiles, CHUNKS)),
         ],
         name="finish",
         compiler_params=LIMIT,

time: 70.9 us -> 70.8 us (level)
  no operation moved by 1% of the time
where the time goes in v4:
time: 70.8 us; the launch traced here: 70.4 us
  Pallas kernels  30.3 us (43%)
  waiting for transfers between devices  23.4 us (33%)
  starting transfers between devices  15.8 us (22%)
  between operations  0.82 us (1%)
    all_to_all x2, waiting for transfers between devices, exchange(): return lax.all_to_all(x, AXES, split_axis=0, concat_axis=0, tiled=True)  23.4 us
    all_to_all x2, starting transfers between devices, exchange(): return lax.all_to_all(x, AXES, split_axis=0, concat_axis=0, tiled=True)  15.8 us
    pallas_call x1, Pallas kernels, make_base(): pl.pallas_call(base_kernel, grid=(boxes // TILE,), in_specs=[smem, smem,...  15.1 us
    pallas_call x1, Pallas kernels, finish(): pl.pallas_call(final_kernel, in_specs=[ANYWHERE, VMEM_SPEC, ANYWHERE, ANY...  7.4 us
    pallas_call x1, Pallas kernels, serve(): pl.pallas_call(serve_kernel, in_specs=[ANYWHERE, VMEM_SPEC, VMEM_SPEC], o...  3.89 us
    pallas_call x1, Pallas kernels, route(): pl.pallas_call(route_kernel, in_specs=[vmem, vmem], out_specs=[vmem, vmem...  2.37 us
    pallas_call x1, Pallas kernels, prepare(): pl.pallas_call(prepare_kernel, in_specs=[ANYWHERE] * 3, out_specs=[VMEM_S...  1.61 us
  transfers between devices with their start and end apart: 2, of which 2 were waited for; matrix products, arithmetic and copies ran while one was open for 0% of the time, Pallas kernels for 24%

profile of v4, /device:TPU:1, one launch (start us, length us, event | category | flops | bytes accessed | tf_op | source)
XLA Modules:
  0.0 70.4 jit_solution(12351738242858821054)
XLA Ops:
  0.6 2.4 %route.1 = (s32[128,1,8]{2,1,0:T(1,128)}, s32[2,1024]{1,0:T(2,128)}, f32[2,1024]{1,0:T(2,128)}) custom-call(s32[2,1024]{1,0:T(2,128)} %bitcast.7, s32[1,1024]{1,0:T(1,128)} %bitcast.6), custom_call_target="tpu_custom_call" | custom-call | tf_op jit(solution)/shard_map/route/pallas_call | solution.py:90
  3.0 11.5 %all-to-all-start = ((s32[128,1,8]{2,1,0:T(1,128)}), s32[128,1,8]{2,1,0:T(1,128)S(1)}, u32[]{:S(2)}, u32[]{:S(2)}) async-start(s32[128,1,8]{2,1,0:T(1,128)} %get-tuple-element.10), calls=%async_computation | async-start | bytes 131072 | tf_op jit(solution)/shard_map/all_to_all | solution.py:498
  14.5 1.6 %prepare.1 = (f32[1024,512]{1,0:T(8,128)S(1)}, f32[64,8,128]{2,1,0:T(8,128)S(1)}) custom-call(s32[1024]{0:T(1024)} %mask_ref.3, f32[3,8,8]{2,1,0:T(8,128)} %blocks_ref.3, f32[1024,512]{1,0:T(8,128)} %coef_ref.3), custom_call_target="tpu_custom_call" | custom-call | flops 8388608 | bytes 4194304 | tf_op jit(solution)/shard_map/prepare/pallas_call | solution.py:195
  16.1 7.9 %all-to-all-done.request_ref = s32[128,1,8]{2,1,0:T(1,128)S(1)} async-done(((s32[128,1,8]{2,1,0:T(1,128)}), s32[128,1,8]{2,1,0:T(1,128)S(1)}, u32[]{:S(2)}, u32[]{:S(2)}) %all-to-all-start) | async-done | bytes 4128 | tf_op jit(solution)/shard_map/all_to_all | solution.py:498
  24.1 3.9 %serve.1 = f32[1024,4,128]{2,1,0:T(4,128)} custom-call(s32[128,1,8]{2,1,0:T(1,128)S(1)} %all-to-all-done.request_ref, f32[1024,512]{1,0:T(8,128)S(1)} %get-tuple-element.11.live_ref, f32[64,8,128]{2,1,0:T(8,128)S(1)} %get-tuple-element.12.weight_ref), custom_call_target="tpu_custom_call" | custom-call | tf_op jit(solution)/shard_map/serve/pallas_call | solution.py:252
  28.0 4.3 %all-to-all-start.1 = ((f32[128,32,128]{2,1,0:T(8,128)}), f32[128,32,128]{2,1,0:T(8,128)S(1)}, u32[]{:S(2)}, u32[]{:S(2)}) async-start(f32[128,32,128]{2,1,0:T(8,128)} %bitcast.5), calls=%async_computation.1 | async-start | bytes 4194304 | tf_op jit(solution)/shard_map/all_to_all | solution.py:498
  32.3 15.1 %base.1 = (f32[4096,128]{1,0:T(8,128)}, bf16[4,256,256]{2,1,0:T(8,128)(2,1)}) custom-call(s32[1024]{0:T(1024)} %mask_ref.3, f32[3,8,8]{2,1,0:T(8,128)} %blocks_ref.3, f32[2,1024]{1,0:T(2,128)} %get-tuple-element.13.local_ref, f32[1024,512]{1,0:T(8,128)} %coef_ref.3, f32[16,16]{1,0:T(8,128)} %scale_ref.1), custom_call_target="tpu_custom_call" | custom-call | flops 16777216 | bytes 8388608 | tf_op jit(solution)/shard_map/base/pallas_call | solution.py:335
  47.4 15.5 %all-to-all-done.1 = f32[128,32,128]{2,1,0:T(8,128)S(1)} async-done(((f32[128,32,128]{2,1,0:T(8,128)}), f32[128,32,128]{2,1,0:T(8,128)S(1)}, u32[]{:S(2)}, u32[]{:S(2)}) %all-to-all-start.1) | async-done | bytes 2097184 | tf_op jit(solution)/shard_map/all_to_all | solution.py:498
  62.9 7.4 %finish.1 = (f32[1024,512]{1,0:T(8,128)}, f32[1024,512]{1,0:T(8,128)}) custom-call(s32[2,1024]{1,0:T(2,128)} %get-tuple-element.9.ghost_index_ref, f32[1024,4,128]{2,1,0:T(4,128)S(1)} %bitcast.4, f32[4096,128]{1,0:T(8,128)} %get-tuple-element.14.base_ref, bf16[4,256,256]{2,1,0:T(8,128)(2,1)} %get-tuple-element.15.matrix_ref), custom_call_target="tpu_custom_call" | custom-call | tf_op jit(solution)/shard_map/finish/pallas_call | solution.py:472
Async XLA Ops:
  3.0 21.1 %all-to-all-start = ((s32[128,1,8]{2,1,0:T(1,128)}), s32[128,1,8]{2,1,0:T(1,128)S(1)}, u32[]{:S(2)}, u32[]{:S(2)}) async-start(s32[128,1,8]{2,1,0:T(1,128)} %get-tuple-element.10), calls=%async_computation | async-start | bytes 131072 | tf_op jit(solution)/shard_map/all_to_all | solution.py:498
  28.0 34.9 %all-to-all-start.1 = ((f32[128,32,128]{2,1,0:T(8,128)}), f32[128,32,128]{2,1,0:T(8,128)S(1)}, u32[]{:S(2)}, u32[]{:S(2)}) async-start(f32[128,32,128]{2,1,0:T(8,128)} %bitcast.5), calls=%async_computation.1 | async-start | bytes 4194304 | tf_op jit(solution)/shard_map/all_to_all | solution.py:498
